TPU v7x, 32 devices: a whole 2x2x4 slice. The times are simulated.
32 devices in a mesh: dp: 8 (over z, y), tp: 4 (over x, core).
Axes of the slice: x: 2, y: 2, z: 4, core: 2. Of those that a mesh axis runs over, the one named last changes fastest.
Arguments:
- query_latent: bfloat16 [3, 128, 128, 512], P(None, 'dp', 'tp'), may hold values from -18 to 18
- query_rotary: bfloat16 [3, 128, 128, 64], P(None, 'dp', 'tp'), may hold values from -18 to 18
- token_latent: bfloat16 [3, 128, 512], P(None, 'dp', 'tp'), may hold values from -5 to 5
- token_rotary: bfloat16 [3, 128, 64], P(None, 'dp', 'tp'), may hold values from -5 to 5
- cache_latent: bfloat16 [96, 8, 128, 512], P('dp'), may hold values from -6 to 6
- cache_rotary: bfloat16 [96, 8, 64, 128], P('dp'), may hold values from -6 to 6
- cache_exponent: int32 [96, 8, 5], P('dp'), may hold values from -1 to 1
- handed_latent: bfloat16 [256, 128, 512], P('dp'), may hold values from -6 to 6
- handed_rotary: bfloat16 [256, 64, 128], P('dp'), may hold values from -6 to 6
- handed_exponent: int32 [256, 5], P('dp'), may hold values from -1 to 1
- block_request: int32 [256], P('dp'), may hold values from -1 to 127, as said below
- block_index: int32 [256], P('dp'), may hold values from -1 to 7, as said below
- lengths: int32 [128], P('dp'), may hold values from 1 to 1024, as said below
- value_up: bfloat16 [128, 512, 128], P('tp'), may hold values from -0.25 to 0.25
Outputs:
- attended: bfloat16 [3, 128, 16384], P(None, 'dp', 'tp')
Inputs may be any that keep to these rules, and one draw needn't show every extreme that they name: `lengths`: requests g with g % 16 < 12 have resident cache, the others prefill blocks; some request of the latter kind has the largest length. `block_request`: -1 marks an empty slot; otherwise a request with g % 16 >= 12. Each of its blocks 0 to ceil(lengths[g] / 128) - 1 is in exactly one slot. The 32 slots of one dp index hold at most 4 blocks of the requests of any one owner g // 16; in every draw some owner gets exactly 4 from every dp index. `block_index`: -1 exactly in empty slots.
All inputs are finite; a program needn't handle non-finite values.
Results may differ from a plain program's by a relative error of at most 0.0052.
Values may be sent and summed in bfloat16 or wider, within the bound.
A program may use at most 128 MiB of HBM per device.

v0:
```python
import jax
import jax.numpy as jnp
from jax import lax
from jax.sharding import PartitionSpec as P

GROUP = 128


score_scale = 192.0 ** (-0.5)
masked_score = -1e30


def local(
    query_latent,
    query_rotary,
    token_latent,
    token_rotary,
    cache_latent,
    cache_rotary,
    cache_exponent,
    handed_latent,
    handed_rotary,
    handed_exponent,
    block_request,
    block_index,
    lengths,
    value_up,
):
    owners = lax.axis_size("dp")
    req_dev = lengths.shape[0]
    res_dev, nb_max, block_rows, width = cache_latent.shape
    src_blk = block_request.shape[0]
    capacity = src_blk // owners
    steps_count = query_latent.shape[0]
    token_all, token_rot = (
        lax.all_gather(token_latent, "tp", axis=2, tiled=True),
        lax.all_gather(token_rotary, "tp", axis=2, tiled=True),
    )
    target = jnp.where(block_request >= 0, block_request // req_dev, -1)
    slot_ids = jnp.arange(src_blk)
    before = slot_ids[None, :] < slot_ids[:, None]
    arrival = jnp.sum((before & (target[None, :] == target[:, None])).astype(jnp.int32), axis=1)
    picks = (target[None, None, :] == jnp.arange(owners)[:, None, None]) & (
        arrival[None, None, :] == jnp.arange(capacity)[None, :, None]
    )
    source = jnp.sum(jnp.where(picks, slot_ids[None, None, :], 0), axis=2)
    filled = jnp.any(picks, axis=2).astype(jnp.int32)
    requested = block_request % req_dev
    details = jnp.concatenate(
        [
            jnp.stack([filled, requested[source], block_index[source]], axis=-1),
            handed_exponent[source],
        ],
        axis=-1,
    )
    latent_send = handed_latent[source]
    rotary_send = handed_rotary[source]
    got_latent, got_rotary, arrived = (
        lax.all_to_all(latent_send, "dp", split_axis=0, concat_axis=0, tiled=True),
        lax.all_to_all(rotary_send, "dp", split_axis=0, concat_axis=0, tiled=True),
        lax.all_to_all(details, "dp", split_axis=0, concat_axis=0, tiled=True),
    )
    resident_count = res_dev * nb_max
    received = owners * capacity
    all_latent = jnp.concatenate(
        [
            cache_latent.reshape(resident_count, block_rows, width),
            got_latent.reshape(received, block_rows, width),
        ],
        axis=0,
    )
    all_rotary = jnp.concatenate(
        [
            cache_rotary.reshape(resident_count, cache_rotary.shape[2], block_rows),
            got_rotary.reshape(received, got_rotary.shape[2], block_rows),
        ],
        axis=0,
    )
    arrived = arrived.reshape(received, arrived.shape[-1])
    exponents = jnp.concatenate(
        [cache_exponent.reshape(resident_count, cache_exponent.shape[-1]), arrived[:, 3:]], axis=0
    )
    slot_request = jnp.concatenate(
        [jnp.repeat(jnp.arange(res_dev, dtype=jnp.int32), nb_max), arrived[:, 1]]
    )
    slot_index = jnp.concatenate(
        [jnp.tile(jnp.arange(nb_max, dtype=jnp.int32), res_dev), arrived[:, 2]]
    )
    slot_live = jnp.concatenate([jnp.ones((resident_count,), bool), arrived[:, 0] == 1])
    factors = jnp.exp2(exponents.astype(jnp.float32)).astype(jnp.bfloat16)
    columns = jnp.repeat(factors[:, :-1], GROUP, axis=1)
    keys_all = all_latent * columns[:, None, :]
    keys_rot = all_rotary * factors[:, -1:, None]
    slot_query = jnp.take(query_latent, slot_request, axis=1)
    slot_rotary = jnp.take(query_rotary, slot_request, axis=1)
    scores = jnp.einsum("sqhc,qkc->sqhk", slot_query, keys_all, preferred_element_type=jnp.float32)
    scores = (
        scores
        + jnp.einsum("sqhd,qdk->sqhk", slot_rotary, keys_rot, preferred_element_type=jnp.float32)
    ) * score_scale
    positions = slot_index[:, None] * block_rows + jnp.arange(block_rows)[None, :]
    visible = slot_live[:, None] & (positions < jnp.take(lengths, slot_request)[:, None])
    scores = jnp.where(visible[None, :, None, :], scores, masked_score)
    slot_peak = jnp.max(scores, axis=-1)
    member = slot_request[:, None] == jnp.arange(req_dev)[None, :]
    cache_peak = jnp.max(
        jnp.where(member[None, :, :, None], slot_peak[:, :, None, :], masked_score), axis=1
    )
    fresh = jnp.einsum(
        "srhc,trc->srht", query_latent, token_all, preferred_element_type=jnp.float32
    )
    fresh = (
        fresh
        + jnp.einsum("srhd,trd->srht", query_rotary, token_rot, preferred_element_type=jnp.float32)
    ) * score_scale
    step_ids = jnp.arange(steps_count)
    fresh = jnp.where(
        (step_ids[None, :] <= step_ids[:, None])[:, None, None, :], fresh, masked_score
    )
    peak = jnp.maximum(cache_peak, jnp.max(fresh, axis=-1))
    weights = jnp.exp(scores - jnp.take(peak, slot_request, axis=1)[..., None])
    slot_total = jnp.sum(weights, axis=-1)
    partial_sums = jnp.einsum(
        "sqhk,qkc->sqhc", weights.astype(jnp.bfloat16), keys_all, preferred_element_type=jnp.float32
    )
    one_hot = member.astype(jnp.float32)
    summed = jnp.einsum("sqhc,qr->srhc", partial_sums, one_hot, precision=lax.Precision.HIGHEST)
    total = jnp.einsum("sqh,qr->srh", slot_total, one_hot, precision=lax.Precision.HIGHEST)
    fresh_weights = jnp.exp(fresh - peak[..., None])
    total = total + jnp.sum(fresh_weights, axis=-1)
    summed = summed + jnp.einsum(
        "srht,trc->srhc",
        fresh_weights.astype(jnp.bfloat16),
        token_all,
        preferred_element_type=jnp.float32,
    )
    mixed = (summed / total[..., None]).astype(jnp.bfloat16)
    output = jnp.einsum(
        "srhc,hcv->srhv", mixed, value_up, preferred_element_type=jnp.float32
    ).astype(jnp.bfloat16)
    return output.reshape(steps_count, req_dev, -1)


def solution(mesh):
    placed = (
        P(None, "dp", "tp", None),
        P(None, "dp", "tp", None),
        P(None, "dp", "tp"),
        P(None, "dp", "tp"),
        P("dp", None, None, None),
        P("dp", None, None, None),
        P("dp", None, None),
        P("dp", None, None),
        P("dp", None, None),
        P("dp", None),
        P("dp"),
        P("dp"),
        P("dp"),
        P("tp", None, None),
    )
    return jax.shard_map(
        local, mesh=mesh, in_specs=placed, out_specs=P(None, "dp", "tp"), check_vma=False
    )
```

profile of v0, /device:TPU:25, one launch (start us, length us, event | category | flops | bytes accessed | tf_op | source)
XLA Modules:
  0.0 213.5 jit_solution(15775459415264868811)
XLA Ops:
  0.0 0.8 and_select_fusion.1
  0.8 0.2 convert_reduce_fusion
  1.0 0.2 fusion.72
  1.2 0.2 and_reduce_fusion
  1.5 0.7 gather_fusion
  2.2 0.1 stack.9
  2.3 0.8 copy.104
  3.1 0.6 gather_fusion.2
  3.7 0.7 gather_fusion.1
  4.4 0.1 stack.10
  4.5 0.1 copy.105
  4.6 0.7 pad_add_fusion
  5.3 5.5 %all-to-all-start = ((s32[8,4,8]{2,1,0:T(4,128)}), s32[8,4,8]{2,1,0:T(4,128)S(1)}, u32[]{:S(2)}, u32[]{:S(2)}) async-start(s32[8,4,8]{2,1,0:T(4,128)} %pad_add_fusion), calls=%async_computation | async-start | bytes 32768 | tf_op jit(solution)/shard_map/all_to_all | solution.py:61
  10.8 1.4 gather_fusion.5
  12.2 1.2 all-to-all-done
  13.5 6.2 %all-to-all-start.2 = ((bf16[8,4,64,128]{3,2,1,0:T(8,128)(2,1)}), bf16[8,4,64,128]{3,2,1,0:T(8,128)(2,1)S(1)}, u32[]{:S(2)}, u32[]{:S(2)}) async-start(bf16[8,4,64,128]{3,2,1,0:T(8,128)(2,1)} %bitcast.30), calls=%async_computation.2 | async-start | bytes 1048576 | tf_op jit(solution)/shard_map/all_to_all | solution.py:60
  19.7 5.0 %gather_fusion.3 = bf16[32,128,512]{2,1,0:T(8,128)(2,1)} fusion(bf16[32,128,512]{2,1,0:T(8,128)(2,1)} %param.21, s32[1024]{0:T(1024)S(1)} %pad_clamp_fusion.1), kind=kCustom, calls=%fused_computation.3 | custom fusion | bytes 8388736 | tf_op jit(solution)/shard_map/gather | solution.py:56
  24.7 6.2 %all-to-all-done.2 = bf16[8,4,64,128]{3,2,1,0:T(8,128)(2,1)S(1)} async-done(((bf16[8,4,64,128]{3,2,1,0:T(8,128)(2,1)}), bf16[8,4,64,128]{3,2,1,0:T(8,128)(2,1)S(1)}, u32[]{:S(2)}, u32[]{:S(2)}) %all-to-all-start.2) | async-done | bytes 524320 | tf_op jit(solution)/shard_map/all_to_all | solution.py:60
  30.9 6.3 %all-to-all-start.1 = ((bf16[8,4,128,512]{3,2,1,0:T(8,128)(2,1)}), bf16[8,4,128,512]{3,2,1,0:T(8,128)(2,1)}, u32[]{:S(2)}, u32[]{:S(2)}) async-start(bf16[8,4,128,512]{3,2,1,0:T(8,128)(2,1)} %bitcast.127), calls=%async_computation.1 | async-start | bytes 8388608 | tf_op jit(solution)/shard_map/all_to_all | solution.py:59
  37.3 0.1 copy.108
  37.7 7.8 %all_gather.7 = bf16[3,16,64]{1,0,2:T(4,128)(2,1)S(1)} all-gather(bf16[3,16,16]{1,0,2:T(4,128)(2,1)S(1)} %copy.115), channel_id=1, replica_groups=mesh['dp'=8,'tp'=4] {'tp'}, dimensions={2}, use_global_device_ids=true | all-gather | bytes 7680 | tf_op jit(solution)/shard_map/all_gather | solution.py:37
  45.6 0.1 copy.128
  45.7 5.3 %all_gather.6 = bf16[3,16,512]{2,0,1:T(4,128)(2,1)S(1)} all-gather(bf16[3,16,128]{2,0,1:T(4,128)(2,1)S(1)} %copy.113), channel_id=1, replica_groups=mesh['dp'=8,'tp'=4] {'tp'}, dimensions={2}, use_global_device_ids=true | all-gather | bytes 61440 | tf_op jit(solution)/shard_map/all_gather | solution.py:36
  50.9 0.7 fusion.90
  51.7 0.5 fusion.61
  52.2 1.0 fusion.91
  53.2 0.2 slice_reduce_fusion
  53.4 10.0 %fusion.82 = (s32[128]{0:T(128)S(1)}, s32[128]{0:T(128)S(1)}, s32[128]{0:T(128)S(1)}) fusion(s32[]{:T(128)} %bitcast.11, s32[]{:T(128)} %bitcast.12, s32[]{:T(128)} %bitcast.13, s32[]{:T(128)} %bitcast.14, s32[]{:T(128)} %bitcast.15, s32[]{:T(128)} %bitcast.16, s32[]{:T(128)} %bitcast.17, s32[]{:T(128)} %bitcast.18, s32[]{:T(128)} %bitcast.19, s32[]{:T(128)} %bitcast.20, ...), kind=kLoop, calls=%fused_computation.120 | loop fusion | flops 5376 | bytes 2624 | tf_op jit(solution)/shard_map/jit(_take)/select_n | solution.py:102
  63.5 8.3 %gather_fusion.4 = bf16[128,3,32,512]{3,2,1,0:T(8,128)(2,1)} fusion(bf16[3,16,32,512]{3,2,1,0:T(8,128)(2,1)S(1)} %copy-done, s32[1024]{0:T(1024)S(1)} %pad_clamp_fusion), kind=kCustom, calls=%fused_computation.4 | custom fusion | bytes 25166336 | tf_op jit(solution)/shard_map/jit(_take)/gather | solution.py:94
  71.8 2.6 %gather_fusion.6 = bf16[128,3,32,64]{3,2,1,0:T(8,128)(2,1)} fusion(bf16[3,16,32,64]{3,2,1,0:T(8,128)(2,1)S(1)} %copy-done.3, s32[1024]{0:T(1024)S(1)} %pad_clamp_fusion), kind=kCustom, calls=%fused_computation.6 | custom fusion | bytes 3146240 | tf_op jit(solution)/shard_map/jit(_take)/gather | solution.py:95
  74.7 0.1 copy.110
  74.8 0.2 broadcast_in_dim.136
  75.0 0.1 fusion.74
  75.3 0.1 fusion.69
  75.5 5.6 %fusion.23 = f32[128,128,3,32]{1,3,2,0:T(8,128)} fusion(bf16[128,3,32,64]{3,2,1,0:T(8,128)(2,1)} %gather_fusion.6, pred[128]{0:T(512)(128)(4,1)S(1)} %compare_and_fusion, bf16[32,64,128]{2,1,0:T(8,128)(2,1)S(1)} %bitcast.128, bf16[96,64,128]{2,1,0:T(8,128)(2,1)S(1)} %bitcast.129, bf16[128]{0:T(256)(128)(2,1)S(1)} %slice_bitcast_fusion), kind=kOutput, calls=%fused_computation.31 | convolution fusion | flops 208404480 | bytes 9961856 | tf_op jit(solution)/shard_map/sqhd,qdk->sqhk/dot_general | solution.py:99
  81.1 48.5 %all-to-all-done.1 = bf16[8,4,128,512]{3,2,1,0:T(8,128)(2,1)} async-done(((bf16[8,4,128,512]{3,2,1,0:T(8,128)(2,1)}), bf16[8,4,128,512]{3,2,1,0:T(8,128)(2,1)}, u32[]{:S(2)}, u32[]{:S(2)}) %all-to-all-start.1) | async-done | bytes 4194336 | tf_op jit(solution)/shard_map/all_to_all | solution.py:59
  129.6 19.4 %bitcast_reduce_fusion = (f32[3,128,32]{2,0,1:T(4,128)S(1)}, f32[128,128,3,32]{1,3,2,0:T(8,128)}) fusion(f32[128,128,3,32]{1,3,2,0:T(8,128)} %fusion.23, bf16[128,3,32,512]{3,2,1,0:T(8,128)(2,1)} %gather_fusion.4, pred[128]{0:T(512)(128)(4,1)S(1)} %compare_and_fusion, bf16[32,128,512]{2,1,0:T(8,128)(2,1)} %bitcast.7, bf16[96,128,512]{2,1,0:T(8,128)(2,1)} %bitcast.138, ...), kind=kOutput, calls=%fused_computation.21 | convolution fusion | flops 1673515008 | bytes 42139776 | tf_op jit(solution)/shard_map/sqhc,qkc->sqhk/dot_general | solution.py:96
  149.1 0.3 select_reduce_fusion
  149.4 0.8 gather_fusion.7
  150.2 0.2 select_bitcast_fusion
  150.4 5.7 %fusion.17 = f32[3,128,32]{2,0,1:T(4,128)S(1)} fusion(f32[128,128,3,32]{1,3,2,0:T(8,128)} %get-tuple-element.32, f32[3,128,32]{2,0,1:T(4,128)S(1)} %select_bitcast_fusion), kind=kLoop, calls=%fused_computation.25 | loop fusion | flops 3133440 | bytes 6389760 | tf_op jit(solution)/shard_map/reduce_sum | solution.py:122
  156.1 21.3 %fusion.10 = f32[3,128,32,512]{3,2,0,1:T(8,128)} fusion(bf16[32,128,512]{2,1,0:T(8,128)(2,1)} %bitcast.7, bf16[96,128,512]{2,1,0:T(8,128)(2,1)} %bitcast.139, bf16[128,512]{1,0:T(8,128)(2,1)S(1)} %bitcast.136, f32[128,128,3,32]{1,3,2,0:T(8,128)} %get-tuple-element.32, f32[3,128,32]{2,0,1:T(4,128)S(1)} %select_bitcast_fusion), kind=kOutput, calls=%fused_computation.17 | convolution fusion | flops 1664090112 | bytes 48414720 | tf_op jit(solution)/shard_map/sqhk,qkc->sqhc/dot_general | solution.py:123
  177.3 0.1 fusion.64
  177.4 2.4 %fusion.66 = f32[16,3,32,512]{3,2,1,0:T(8,128)} fusion(bf16[3,16,512]{2,0,1:T(4,128)(2,1)S(1)} %all_gather.6, f32[3,16,32,3]{2,3,0,1:T(4,128)S(1)} %get-tuple-element.30, f32[3,16,32]{2,0,1:T(4,128)S(1)} %copy_maximum_fusion), kind=kOutput, calls=%fused_computation.63 | convolution fusion | flops 4727808 | bytes 3219456 | tf_op jit(solution)/shard_map/srht,trc->srhc/dot_general | solution.py:131
  179.8 0.2 fusion.59
  180.1 31.7 %fusion.22 = bf16[3,16,32,512]{3,1,0,2:T(8,128)(2,1)S(1)} fusion(f32[16,3,32,512]{3,2,1,0:T(8,128)} %fusion.66, f32[3,128,32,512]{3,2,0,1:T(8,128)} %fusion.10, f32[3,16,32]{1,0,2:T(4,128)S(1)} %copy.123, s32[128]{0:T(128)S(1)} %get-tuple-element.8), kind=kOutput, calls=%fused_computation.30 | convolution fusion | flops 1210320896 | bytes 29891072 | tf_op jit(solution)/shard_map/sqhc,qr->srhc/dot_general | solution.py:127
  211.9 0.8 fusion.44
  212.7 0.8 copy.161
  (54 shorter events, 1.4 us)
Async XLA Ops:
  0.0 52.2 %copy-start = (bf16[3,16,32,512]{3,2,1,0:T(8,128)(2,1)S(1)}, bf16[3,16,32,512]{3,2,1,0:T(8,128)(2,1)}, u32[]{:S(2)}) copy-start(bf16[3,16,32,512]{3,2,1,0:T(8,128)(2,1)} %param.14) | copy-start | bytes 4718596
  0.0 3.7 %copy-start.2 = (s32[32]{0:T(128)S(1)}, s32[32]{0:T(128)}, u32[]{:S(2)}) copy-start(s32[32]{0:T(128)} %param.25) | copy-start | bytes 388
  0.0 10.8 %copy-start.6 = (bf16[32,64,128]{2,1,0:T(8,128)(2,1)S(1)}, bf16[32,64,128]{2,1,0:T(8,128)(2,1)}, u32[]{:S(2)}) copy-start(bf16[32,64,128]{2,1,0:T(8,128)(2,1)} %param.22) | copy-start | bytes 1572868
  5.3 8.1 %all-to-all-start = ((s32[8,4,8]{2,1,0:T(4,128)}), s32[8,4,8]{2,1,0:T(4,128)S(1)}, u32[]{:S(2)}, u32[]{:S(2)}) async-start(s32[8,4,8]{2,1,0:T(4,128)} %pad_add_fusion), calls=%async_computation | async-start | bytes 32768 | tf_op jit(solution)/shard_map/all_to_all | solution.py:61
  13.5 17.4 %all-to-all-start.2 = ((bf16[8,4,64,128]{3,2,1,0:T(8,128)(2,1)}), bf16[8,4,64,128]{3,2,1,0:T(8,128)(2,1)S(1)}, u32[]{:S(2)}, u32[]{:S(2)}) async-start(bf16[8,4,64,128]{3,2,1,0:T(8,128)(2,1)} %bitcast.30), calls=%async_computation.2 | async-start | bytes 1048576 | tf_op jit(solution)/shard_map/all_to_all | solution.py:60
  24.7 12.7 %copy-start.8 = (s32[12,8,5]{0,1,2:T(8,128)S(1)}, s32[12,8,5]{0,1,2:T(8,128)}, u32[]{:S(2)}) copy-start(s32[12,8,5]{0,1,2:T(8,128)} %param.20) | copy-start | bytes 5764
  24.7 13.0 %copy-start.9 = (bf16[3,16,128]{2,1,0:T(8,128)(2,1)S(1)}, bf16[3,16,128]{2,1,0:T(8,128)(2,1)}, u32[]{:S(2)}) copy-start(bf16[3,16,128]{2,1,0:T(8,128)(2,1)} %param.16) | copy-start | bytes 36868
  24.7 13.0 %copy-start.10 = (bf16[3,16,16]{2,1,0:T(8,128)(2,1)S(1)}, bf16[3,16,16]{2,1,0:T(8,128)(2,1)}, u32[]{:S(2)}) copy-start(bf16[3,16,16]{2,1,0:T(8,128)(2,1)} %param.17) | copy-start | bytes 4612
  24.7 26.3 %copy-start.7 = (s32[16]{0:T(128)S(1)}, s32[16]{0:T(128)}, u32[]{:S(2)}) copy-start(s32[16]{0:T(128)} %param.26) | copy-start | bytes 196
  24.7 27.0 %copy-start.3 = (bf16[3,16,32,64]{3,2,1,0:T(8,128)(2,1)S(1)}, bf16[3,16,32,64]{3,2,1,0:T(8,128)(2,1)}, u32[]{:S(2)}) copy-start(bf16[3,16,32,64]{3,2,1,0:T(8,128)(2,1)} %param.15) | copy-start | bytes 589828
  30.9 98.7 %all-to-all-start.1 = ((bf16[8,4,128,512]{3,2,1,0:T(8,128)(2,1)}), bf16[8,4,128,512]{3,2,1,0:T(8,128)(2,1)}, u32[]{:S(2)}, u32[]{:S(2)}) async-start(bf16[8,4,128,512]{3,2,1,0:T(8,128)(2,1)} %bitcast.127), calls=%async_computation.1 | async-start | bytes 8388608 | tf_op jit(solution)/shard_map/all_to_all | solution.py:59
  71.8 3.7 %copy-start.5 = (bf16[12,8,64,128]{3,2,1,0:T(8,128)(2,1)S(1)}, bf16[12,8,64,128]{3,2,1,0:T(8,128)(2,1)}, u32[]{:S(2)}) copy-start(bf16[12,8,64,128]{3,2,1,0:T(8,128)(2,1)} %param.19) | copy-start | bytes 4718596
  180.1 31.7 %copy-start.4 = (bf16[32,512,128]{2,1,0:T(8,128)(2,1)S(1)}, bf16[32,512,128]{2,1,0:T(8,128)(2,1)}, u32[]{:S(2)}) copy-start(bf16[32,512,128]{2,1,0:T(8,128)(2,1)} %param.27) | copy-start | bytes 12582916
  180.1 33.3 %copy-start.1 = (bf16[3,16,32,512]{3,2,1,0:T(8,128)(2,1)S(1)}, bf16[3,16,32,512]{3,2,1,0:T(8,128)(2,1)}, u32[]{:S(2)}) copy-start(bf16[3,16,32,512]{3,2,1,0:T(8,128)(2,1)} %param.14) | copy-start | bytes 4718596
where the time goes:
time: 217 us; the launch traced here: 213 us
  matrix products  82.9 us (38%)
  waiting for transfers between devices  55.9 us (26%)
  local copies, waits for them, and re-layouts  24.6 us (11%)
  other arithmetic  18.8 us (9%)
  starting transfers between devices  18 us (8%)
  blocking collectives  13.1 us (6%)
    all_to_all x1, waiting for transfers between devices, local(): lax.all_to_all(latent_send, 'dp', split_axis=0, concat_axis=0, tiled=True)  48.5 us
    dot_general x1, matrix products, local(): jnp.einsum('sqhc,qr->srhc', partial_sums, one_hot, precision=lax.Precisio...  31.7 us
    dot_general x1, matrix products, local(): jnp.einsum('sqhk,qkc->sqhc', weights.astype(jnp.bfloat16), keys_all, pref...  21.3 us
    dot_general x1, matrix products, local(): jnp.einsum('sqhc,qkc->sqhk', slot_query, keys_all, preferred_element_type...  19.4 us
    select_n x1, other arithmetic, local(): jnp.take(lengths, slot_request)[:, None]  10 us
    gather x1, local copies, waits for them, and re-layouts, local(): slot_query = jnp.take(query_latent, slot_request, axis=1)  8.32 us
    all_gather x1, blocking collectives, local(): lax.all_gather(token_rotary, 'tp', axis=2, tiled=True)  7.82 us
    all_to_all x1, starting transfers between devices, local(): lax.all_to_all(latent_send, 'dp', split_axis=0, concat_axis=0, tiled=True)  6.27 us
  transfers between devices with their start and end apart: 3, of which 3 were waited for; matrix products, arithmetic and copies ran while one was open for 17% of the time, Pallas kernels for 0%

commit v1 on v0

v1 whole, which is shorter than its diff:
```python
import functools

import jax
import jax.numpy as jnp
from jax import lax
from jax.experimental import pallas as pl
from jax.experimental.pallas import tpu as pltpu
from jax.sharding import PartitionSpec as P

GROUP = 128
FIELDS = 16
LANES = 128
MESH = pl.DeviceIdType.MESH

score_scale = 192.0 ** (-0.5)
masked_score = -1e30
VMEM_LIMIT = 48 * 1024 * 1024


def pack_kernel(req_dev, res_dev, request_ref, index_ref, exponent_ref, latent_ref, rotary_ref,
                send_latent, send_rotary, meta, count, sems):
    owners, rows, _ = send_latent.shape
    rot_rows = send_rotary.shape[1]
    src_blk = request_ref.shape[0]
    cap = src_blk // owners
    per_block = latent_ref.shape[1] // rows
    t = lax.axis_index("tp")

    @pl.loop(0, owners)
    def _(o):
        count[o] = 0
        for k in range(cap):
            meta[o, 0, k * FIELDS] = 0
            meta[o, 0, k * FIELDS + 3] = 0

    @pl.loop(0, src_blk)
    def _(slot):
        request = request_ref[slot]

        @pl.when(request >= 0)
        def _():
            o = lax.div(request, req_dev)
            k = count[o]
            count[o] = k + 1
            base = k * FIELDS
            meta[o, 0, base] = 1
            meta[o, 0, base + 1] = request - o * req_dev - res_dev
            meta[o, 0, base + 2] = index_ref[slot]
            meta[o, 0, base + 3] = slot
            for g in range(exponent_ref.shape[1]):
                meta[o, 0, base + 4 + g] = exponent_ref[slot, g]

    block = lax.div(t, per_block)
    piece = lax.rem(t, per_block)
    copies = []
    for o in range(owners):
        slot = meta[o, 0, block * FIELDS + 3]
        copies.append(pltpu.make_async_copy(
            latent_ref.at[slot, pl.ds(pl.multiple_of(piece * rows, rows), rows)], send_latent.at[o], sems.at[o, 0]))
        copies.append(pltpu.make_async_copy(
            rotary_ref.at[slot, pl.ds(pl.multiple_of(piece * rot_rows, rot_rows), rot_rows)], send_rotary.at[o], sems.at[o, 1]))
    for copy in copies:
        copy.start()
    for copy in copies:
        copy.wait()


def attend(query, rotary_query, keys_ref, rot_blocks, exponent, length):
    blocks = len(rot_blocks)
    block_rows = rot_blocks[0].shape[1]
    width = keys_ref.shape[1]
    group_of = lax.broadcasted_iota(jnp.int32, (1, width), 1) // GROUP
    rot = []
    for j in range(blocks):
        power = jnp.full((1, width), exponent(j, 0), jnp.int32)
        for g in range(1, width // GROUP):
            power = jnp.where(group_of == g, exponent(j, g), power)
        factor = jnp.exp2(power.astype(jnp.float32)).astype(jnp.bfloat16)
        rows = slice(j * block_rows, (j + 1) * block_rows)
        keys_ref[rows, :] = keys_ref[rows, :] * factor
        rot_power = jnp.full((1, block_rows), exponent(j, width // GROUP), jnp.int32)
        rot.append(rot_blocks[j] * jnp.exp2(rot_power.astype(jnp.float32)).astype(jnp.bfloat16))
    keys = keys_ref[...]
    scores = lax.dot_general(query, keys, (((1,), (1,)), ((), ())), preferred_element_type=jnp.float32)
    scores = scores + jnp.dot(rotary_query, jnp.concatenate(rot, axis=1), preferred_element_type=jnp.float32)
    position = lax.broadcasted_iota(jnp.int32, (1, blocks * block_rows), 1)
    scores = jnp.where(position < length, scores * score_scale, masked_score)
    peak = jnp.max(scores, axis=1, keepdims=True)
    weights = jnp.exp(scores - peak)
    total = jnp.sum(weights, axis=1, keepdims=True)
    mix = jnp.dot(weights.astype(jnp.bfloat16), keys, preferred_element_type=jnp.float32)
    return mix, peak, total


def exchange_kernel(owners, heads_groups, query_ref, rotary_ref, lengths_ref, exponent_ref,
                    cache_latent, cache_rotary, send_latent, send_rotary, send_meta, token_latent, token_rotary,
                    got_latent, got_rotary, got_meta, got_token, got_token_rot, mix_ref, stat_ref,
                    keys, rots, key_sems, own_sems, dp_send, dp_recv, x_send, x_recv, core_send, core_recv,
                    tok_send, tok_recv):
    me, t = lax.axis_index("dp"), lax.axis_index("tp")
    across = heads_groups // 2
    partner = t + 1 - 2 * lax.rem(t, 2)
    res_dev, blocks, block_rows, width = cache_latent.shape

    def peer(o):
        return lax.rem(me + o, owners)

    def origin(o):
        return lax.rem(me + owners - o, owners)

    def part_of(k):
        return lax.rem(t + heads_groups - 2 * k, heads_groups)

    barrier = pltpu.get_barrier_semaphore()
    for o in range(1, owners):
        pl.semaphore_signal(barrier, inc=1, device_id=(peer(o), t), device_id_type=MESH)
    for k in range(1, heads_groups):
        pl.semaphore_signal(barrier, inc=1, device_id=(me, lax.rem(t + k, heads_groups)), device_id_type=MESH)
    pl.semaphore_wait(barrier, owners - 1 + heads_groups - 1)

    def dp_copies(o):
        dst = peer(o)
        pairs = ((send_latent.at[dst], got_latent.at[me, t]), (send_rotary.at[dst], got_rotary.at[me, t]),
                 (send_meta.at[dst], got_meta.at[me]))
        return [pltpu.make_async_remote_copy(a, b, dp_send.at[o, n], dp_recv.at[o, n], device_id=(dst, t),
                                             device_id_type=MESH) for n, (a, b) in enumerate(pairs)]

    def dp_arrivals(o):
        src = origin(o)
        pairs = ((got_latent.at[src, t], 0), (got_rotary.at[src, t], 1), (got_meta.at[src], 2))
        return [pltpu.make_async_remote_copy(a, a, dp_send.at[o, n], dp_recv.at[o, n], device_id=(src, t),
                                             device_id_type=MESH) for a, n in pairs]

    def forward(o, part, to, send, recv):
        src = origin(o)
        return [pltpu.make_async_remote_copy(a.at[src, part], a.at[src, part], send.at[n], recv.at[n],
                                             device_id=(me, to), device_id_type=MESH)
                for n, a in enumerate((got_latent, got_rotary))]

    def x_copies(o, k):
        return forward(o, t, lax.rem(t + 2 * k, heads_groups), x_send.at[o, k - 1], x_recv.at[o, k - 1])

    def x_arrivals(o, k):
        return forward(o, part_of(k), part_of(k), x_send.at[o, k - 1], x_recv.at[o, k - 1])

    def core_copies(o, k):
        return forward(o, part_of(k), partner, core_send.at[o, k], core_recv.at[o, k])

    def core_arrivals(o, k):
        part = lax.rem(partner + heads_groups - 2 * k, heads_groups)
        return forward(o, part, partner, core_send.at[o, k], core_recv.at[o, k])

    def token_copies(k):
        to = lax.rem(t + k, heads_groups)
        return [pltpu.make_async_remote_copy(a, b.at[t], tok_send.at[k, n], tok_recv.at[k, n], device_id=(me, to),
                                             device_id_type=MESH)
                for n, (a, b) in enumerate(((token_latent, got_token), (token_rotary, got_token_rot)))]

    def token_arrivals(k):
        src = lax.rem(t + heads_groups - k, heads_groups)
        return [pltpu.make_async_remote_copy(b.at[src], b.at[src], tok_send.at[k, n], tok_recv.at[k, n],
                                             device_id=(me, src), device_id_type=MESH)
                for n, b in enumerate((got_token, got_token_rot))]

    def cache_copies(i, slot):
        return [pltpu.make_async_copy(cache_latent.at[i], keys.at[slot], key_sems.at[slot, 0]),
                pltpu.make_async_copy(cache_rotary.at[i], rots.at[slot], key_sems.at[slot, 1])]

    for copy in cache_copies(0, 0):
        copy.start()
    for o in range(1, owners):
        for copy in dp_copies(o):
            copy.start()
    own = [pltpu.make_async_copy(send_meta.at[me], got_meta.at[me], own_sems.at[0]),
           pltpu.make_async_copy(token_latent, got_token.at[t], own_sems.at[1]),
           pltpu.make_async_copy(token_rotary, got_token_rot.at[t], own_sems.at[2])]
    for copy in own:
        copy.start()
    for k in range(1, heads_groups):
        for copy in token_copies(k):
            copy.start()

    def first_hop(o):
        for copy in dp_arrivals(o):
            copy.wait_recv()
        for k in range(1, across):
            for copy in x_copies(o, k):
                copy.start()
        for copy in core_copies(o, 0):
            copy.start()

    def second_hop(o):
        for k in range(1, across):
            for copy in x_arrivals(o, k):
                copy.wait_recv()
            for copy in core_copies(o, k):
                copy.start()

    first_at = {}
    second_at = {}
    for o in range(1, owners):
        first_at.setdefault(min(res_dev - 1, 2 + (o * 7) // (owners - 1)), []).append(o)
        second_at.setdefault(min(res_dev - 1, 4 + (o * 7) // (owners - 1)), []).append(o)

    @pl.loop(0, res_dev)
    def _(i):
        slot = lax.rem(i, 2)

        @pl.when(i + 1 < res_dev)
        def _():
            for copy in cache_copies(i + 1, 1 - slot):
                copy.start()

        for copy in cache_copies(i, slot):
            copy.wait()
        steps, _, heads, _ = query_ref.shape
        rows = steps * heads
        query = query_ref[:, i].reshape(rows, width)
        rotary_query = rotary_ref[:, i].reshape(rows, rotary_ref.shape[3])
        key_view = keys.at[slot].reshape(blocks * block_rows, width)
        mix, peak, total = attend(query, rotary_query, key_view, [rots[slot, j] for j in range(blocks)],
                                  lambda j, g: exponent_ref[i, j, g], lengths_ref[i])
        mix_ref[i] = mix
        lane = lax.broadcasted_iota(jnp.int32, (rows, LANES), 1)
        stat_ref[i] = jnp.where(lane == 0, peak, total)
        for at, hops in first_at.items():
            @pl.when(i == at)
            def _(hops=hops):
                for o in hops:
                    first_hop(o)
        for at, hops in second_at.items():
            @pl.when(i == at)
            def _(hops=hops):
                for o in hops:
                    second_hop(o)

    for copy in own:
        copy.wait()
    for k in range(1, heads_groups):
        for copy in token_arrivals(k):
            copy.wait_recv()
        for copy in token_copies(k):
            copy.wait_send()
    for o in range(1, owners):
        for copy in dp_copies(o):
            copy.wait_send()
        for k in range(1, across):
            for copy in x_copies(o, k):
                copy.wait_send()
        for k in range(across):
            for copy in core_copies(o, k):
                copy.wait_send()
            for copy in core_arrivals(o, k):
                copy.wait_recv()


def finish_kernel(query_ref, rotary_ref, lengths_ref, meta, mix_ref, stat_ref, token_ref, token_rot_ref,
                  handed_latent, handed_rotary, got_latent, got_rotary, mixed_ref, keys, rots, powers, sems):
    me = lax.axis_index("dp")
    hand, key_rows, width = keys.shape
    owners, groups, rows, _ = got_latent.shape
    rot_rows = got_rotary.shape[2]
    block_rows = handed_latent.shape[1]
    blocks = key_rows // block_rows
    per_block = block_rows // rows
    cap = groups // per_block
    steps, req_dev, heads, _ = query_ref.shape
    res_dev = req_dev - hand
    groups_of_exponents = width // GROUP + 1

    keys[...] = jnp.zeros_like(keys)
    rots[...] = jnp.zeros_like(rots)

    @pl.loop(0, hand * blocks)
    def _(n):
        for g in range(groups_of_exponents):
            powers[n * 8 + g] = 0

    def each_copy(act):
        @pl.loop(0, owners)
        def _(d):
            for k in range(cap):
                base = k * FIELDS

                @pl.when(meta[d, 0, base] == 1)
                def _(k=k, base=base):
                    i, b, slot = meta[d, 0, base + 1], meta[d, 0, base + 2], meta[d, 0, base + 3]
                    for g in range(groups_of_exponents):
                        powers[(i * blocks + b) * 8 + g] = meta[d, 0, base + 4 + g]
                    for p in range(per_block):
                        at = pl.multiple_of(b * block_rows + p * rows, rows)
                        to_keys = keys.at[i, pl.ds(at, rows)]
                        to_rots = rots.at[i * blocks + b, pl.ds(p * rot_rows, rot_rows)]

                        @pl.when(d == me)
                        def _():
                            act(pltpu.make_async_copy(handed_latent.at[slot, pl.ds(p * rows, rows)], to_keys,
                                                      sems.at[d, k * per_block + p, 0]))
                            act(pltpu.make_async_copy(handed_rotary.at[slot, pl.ds(p * rot_rows, rot_rows)], to_rots,
                                                      sems.at[d, k * per_block + p, 1]))

                        @pl.when(d != me)
                        def _():
                            act(pltpu.make_async_copy(got_latent.at[d, k * per_block + p], to_keys,
                                                      sems.at[d, k * per_block + p, 0]))
                            act(pltpu.make_async_copy(got_rotary.at[d, k * per_block + p], to_rots,
                                                      sems.at[d, k * per_block + p, 1]))

    each_copy(lambda copy: copy.start())

    def add_tokens(r, query, rotary_query, mix, peak, total):
        tokens, token_rot = token_ref[r], token_rot_ref[r]
        nt = (((1,), (1,)), ((), ()))
        fresh = (lax.dot_general(query, tokens, nt, preferred_element_type=jnp.float32)
                 + lax.dot_general(rotary_query, token_rot, nt, preferred_element_type=jnp.float32)) * score_scale
        step = lax.broadcasted_iota(jnp.int32, fresh.shape, 0) // heads
        fresh = jnp.where(lax.broadcasted_iota(jnp.int32, fresh.shape, 1) <= step, fresh, masked_score)
        top = jnp.maximum(peak, jnp.max(fresh, axis=1, keepdims=True))
        fresh = jnp.exp(fresh - top)
        shrink = jnp.exp(peak - top)
        total = total * shrink + jnp.sum(fresh, axis=1, keepdims=True)
        mix = mix * shrink + jnp.dot(fresh.astype(jnp.bfloat16), tokens, preferred_element_type=jnp.float32)
        mixed_ref[:, r] = (mix / total).astype(jnp.bfloat16).reshape(steps, heads, width)

    def queries(r):
        return (query_ref[:, r].reshape(steps * heads, width),
                rotary_ref[:, r].reshape(steps * heads, rotary_ref.shape[3]))

    @pl.loop(0, res_dev)
    def _(r):
        query, rotary_query = queries(r)
        add_tokens(r, query, rotary_query, mix_ref[r], stat_ref[r][:, 0:1], stat_ref[r][:, 1:2])

    each_copy(lambda copy: copy.wait())

    @pl.loop(0, hand)
    def _(i):
        query, rotary_query = queries(res_dev + i)
        mix, peak, total = attend(query, rotary_query, keys.at[i], [rots[i * blocks + j] for j in range(blocks)],
                                  lambda j, g: powers[(i * blocks + j) * 8 + g], lengths_ref[res_dev + i])
        add_tokens(res_dev + i, query, rotary_query, mix, peak, total)


def local(
    query_latent,
    query_rotary,
    token_latent,
    token_rotary,
    cache_latent,
    cache_rotary,
    cache_exponent,
    handed_latent,
    handed_rotary,
    handed_exponent,
    block_request,
    block_index,
    lengths,
    value_up,
):
    owners, groups = lax.axis_size("dp"), lax.axis_size("tp")
    req_dev = lengths.shape[0]
    res_dev, blocks, block_rows, width = cache_latent.shape
    rot_width = cache_rotary.shape[2]
    hand = req_dev - res_dev
    src_blk = block_request.shape[0]
    cap = src_blk // owners
    steps, _, heads, _ = query_latent.shape
    rows, rot_rows = cap * block_rows // groups, cap * rot_width // groups
    across = groups // 2
    bf16, f32 = jnp.bfloat16, jnp.float32
    shape = jax.ShapeDtypeStruct
    hbm, vmem, smem = (pl.BlockSpec(memory_space=m) for m in (pl.ANY, pltpu.VMEM, pltpu.SMEM))
    dma = pltpu.SemaphoreType.DMA

    send_latent, send_rotary, send_meta = pl.pallas_call(
        functools.partial(pack_kernel, req_dev, res_dev),
        out_shape=[shape((owners, rows, width), bf16), shape((owners, rot_rows, block_rows), bf16),
                   shape((owners, 1, LANES), jnp.int32)],
        in_specs=[smem, smem, smem, hbm, hbm],
        out_specs=[hbm, hbm, smem],
        scratch_shapes=[pltpu.SMEM((owners,), jnp.int32), dma((owners, 2))],
        name="pack",
    )(block_request, block_index, handed_exponent, handed_latent, handed_rotary)

    got_latent, got_rotary, got_meta, got_token, got_token_rot, mix, stat = pl.pallas_call(
        functools.partial(exchange_kernel, owners, groups),
        out_shape=[shape((owners, groups, rows, width), bf16), shape((owners, groups, rot_rows, block_rows), bf16),
                   shape((owners, 1, LANES), jnp.int32), shape((groups,) + token_latent.shape, bf16),
                   shape((groups,) + token_rotary.shape, bf16), shape((res_dev, steps * heads, width), f32),
                   shape((res_dev, steps * heads, LANES), f32)],
        in_specs=[vmem, vmem, smem, smem] + [hbm] * 7,
        out_specs=[hbm] * 5 + [vmem, vmem],
        scratch_shapes=[pltpu.VMEM((2, blocks, block_rows, width), bf16),
                        pltpu.VMEM((2, blocks, rot_width, block_rows), bf16),
                        dma((2, 2)), dma((3,)), dma((owners, 3)), dma((owners, 3)),
                        dma((owners, across - 1, 2)), dma((owners, across - 1, 2)),
                        dma((owners, across, 2)), dma((owners, across, 2)),
                        dma((groups, 2)), dma((groups, 2))],
        compiler_params=pltpu.CompilerParams(collective_id=0, has_side_effects=True, vmem_limit_bytes=VMEM_LIMIT),
        name="exchange",
    )(query_latent, query_rotary, lengths, cache_exponent, cache_latent, cache_rotary, send_latent, send_rotary,
      send_meta, token_latent, token_rotary)

    def by_request(got):
        whole = jnp.transpose(got, (2, 1, 0, 3)).reshape(req_dev, steps, -1)
        return jnp.pad(whole, ((0, 0), (0, 16 - steps), (0, 0)))

    mixed = pl.pallas_call(
        finish_kernel,
        out_shape=shape((steps, req_dev, heads, width), bf16),
        in_specs=[vmem, vmem, smem, smem, vmem, vmem, vmem, vmem, hbm, hbm, hbm, hbm],
        out_specs=vmem,
        scratch_shapes=[pltpu.VMEM((hand, blocks * block_rows, width), bf16),
                        pltpu.VMEM((hand * blocks, rot_width, block_rows), bf16),
                        pltpu.SMEM((hand * blocks * 8,), jnp.int32), dma((owners, groups, 2))],
        compiler_params=pltpu.CompilerParams(vmem_limit_bytes=VMEM_LIMIT),
        name="finish",
    )(query_latent, query_rotary, lengths, got_meta, mix, stat, by_request(got_token), by_request(got_token_rot),
      handed_latent, handed_rotary, got_latent, got_rotary)

    output = jnp.einsum("srhc,hcv->srhv", mixed, value_up, preferred_element_type=f32).astype(bf16)
    return output.reshape(steps, req_dev, -1)


def solution(mesh):
    placed = (
        P(None, "dp", "tp", None),
        P(None, "dp", "tp", None),
        P(None, "dp", "tp"),
        P(None, "dp", "tp"),
        P("dp", None, None, None),
        P("dp", None, None, None),
        P("dp", None, None),
        P("dp", None, None),
        P("dp", None, None),
        P("dp", None),
        P("dp"),
        P("dp"),
        P("dp"),
        P("tp", None, None),
    )
    return jax.shard_map(
        local, mesh=mesh, in_specs=placed, out_specs=P(None, "dp", "tp"), check_vma=False
    )
```

time: 217 us -> 118 us (0.54); the launches traced: 213 us -> 117 us
  Pallas kernels: 0 us -> 105 us
  matrix products: 82.9 us -> 1.96 us
  waiting for transfers between devices: 55.9 us -> 0 us
  other arithmetic: 18.8 us -> 0 us
  starting transfers between devices: 18 us -> 0 us
  local copies, waits for them, and re-layouts: 24.6 us -> 9.34 us
  blocking collectives: 13.1 us -> 0 us
    pallas_call x0 -> x3, Pallas kernels: none -> 105 us  [the longest x1 50.3 us: local(): pl.pallas_call(functools.partial(exchange_kernel, owners, groups), out_sh...]
    dot_general x9 -> x1, matrix products: 82.9 us -> 1.96 us  [local(): jnp.einsum('srhc,hcv->srhv', mixed, value_up, preferred_element_type=f32)]
    all_to_all x3 -> x0, waiting for transfers between devices: 55.9 us -> none  [the longest x1 48.5 us: local(): lax.all_to_all(latent_send, 'dp', split_axis=0, concat_axis=0, tiled=True)]
    gather x9 -> x0, local copies, waits for them, and re-layouts: 20.7 us -> none  [the longest x1 8.32 us: local(): slot_query = jnp.take(query_latent, slot_request, axis=1)]
    all_to_all x3 -> x0, starting transfers between devices: 18 us -> none  [the longest x1 6.27 us: local(): lax.all_to_all(latent_send, 'dp', split_axis=0, concat_axis=0, tiled=True)]
    all_gather x2 -> x0, blocking collectives: 13.1 us -> none  [the longest x1 7.82 us: local(): lax.all_gather(token_rotary, 'tp', axis=2, tiled=True)]
    select_n x4 -> x0, other arithmetic: 11 us -> none  [the longest x1 10 us: local(): jnp.take(lengths, slot_request)[:, None]]
    unnamed x27 -> x28, local copies, waits for them, and re-layouts: 1.05 us -> 8.31 us
  transfers between devices with their start and end apart: 3 -> 0, of which waited for: 3 -> 0; matrix products, arithmetic and copies ran while one was open for 17% -> 0% of each run, Pallas kernels for 0% -> 0%
where the time goes in v1:
time: 118 us; the launch traced here: 117 us
  Pallas kernels  105 us (89%)
  local copies, waits for them, and re-layouts  9.34 us (8%)
  matrix products  1.96 us (2%)
    pallas_call x1, Pallas kernels, local(): pl.pallas_call(functools.partial(exchange_kernel, owners, groups), out_sh...  50.3 us
    pallas_call x1, Pallas kernels, local(): pl.pallas_call(functools.partial(pack_kernel, req_dev, res_dev), out_shap...  40 us
    pallas_call x1, Pallas kernels, local(): pl.pallas_call(finish_kernel, out_shape=shape((steps, req_dev, heads, wid...  14.9 us
    unnamed x28, local copies, waits for them, and re-layouts  8.31 us

profile of v1, /device:TPU:25, one launch (start us, length us, event | category | flops | bytes accessed | tf_op | source)
XLA Modules:
  0.0 116.7 jit_solution(11105905471514618406)
XLA Ops:
  0.0 1.4 %copy.20.exponent_ref = s32[32,5]{1,0:T(8,128)} copy(s32[32,5]{0,1:T(8,128)} %param.23) | data formatting | bytes 1280 | tf_op args[9]
  1.4 0.9 copy.21.exponent_ref
  2.2 0.0 copy-start
  2.2 0.0 copy-start.3
  2.2 0.0 copy-start.8
  2.2 0.0 copy-start.9
  2.3 0.0 copy-start.11
  2.3 40.0 %pack.1 = (bf16[8,128,512]{2,1,0:T(8,128)(2,1)}, bf16[8,64,128]{2,1,0:T(8,128)(2,1)}, s32[8,1,128]{2,1,0:T(1,128)}) custom-call(s32[32]{0:T(128)} %request_ref.1, s32[32]{0:T(128)} %index_ref.1, s32[32,5]{1,0:T(8,128)} %copy.20.exponent_ref, bf16[32,128,512]{2,1,0:T(8,128)(2,1)} %handed_latent.1, bf16[32,64,128]{2,1,0:T(8,128)(2,1)} %handed_rotary.1), custom_call_target="tpu_custom_call" | custom-call | tf_op jit(solution)/shard_map/pack/pallas_call | solution.py:375
  42.3 0.0 copy-done
  42.3 0.0 copy-done.3
  42.3 0.0 copy-done.8
  42.3 0.0 copy-done.9
  42.3 0.0 copy-done.11
  42.4 0.0 copy-start.2
  42.4 1.4 %copy-done.2 = bf16[12,8,64,128]{3,2,1,0:T(8,128)(2,1)S(1)} copy-done((bf16[12,8,64,128]{3,2,1,0:T(8,128)(2,1)S(1)}, bf16[12,8,64,128]{3,2,1,0:T(8,128)(2,1)}, u32[]{:S(2)}) %copy-start.2) | copy-done | bytes 1572888
  43.8 0.0 copy-start.4
  43.8 1.2 %copy-done.4 = bf16[8,128,512]{2,1,0:T(8,128)(2,1)S(1)} copy-done((bf16[8,128,512]{2,1,0:T(8,128)(2,1)S(1)}, bf16[8,128,512]{2,1,0:T(8,128)(2,1)}, u32[]{:S(2)}) %copy-start.4) | copy-done | bytes 1048600
  45.0 0.0 copy-start.7
  45.0 0.9 copy-done.7
  45.9 0.0 copy-start.10
  45.9 0.7 copy-done.10
  46.6 0.0 copy-start.1
  46.6 50.3 %exchange.1 = (bf16[8,4,128,512]{3,2,1,0:T(8,128)(2,1)}, bf16[8,4,64,128]{3,2,1,0:T(8,128)(2,1)S(1)}, s32[8,1,128]{2,1,0:T(1,128)S(1)}, bf16[4,3,16,128]{3,2,1,0...) custom-call(bf16[3,16,32,512]{3,2,1,0:T(8,128)(2,1)S(1)} %copy-done, ...), custom_call_target="tpu_custom_call" | custom-call | tf_op jit(solution)/shard_map/exchange/pallas_call | solution.py:385
  96.9 0.0 copy-start.5
  96.9 0.8 copy-done.5
  97.8 0.1 reshape.14
  98.0 0.0 copy-done.1
  98.0 0.0 copy-start.6
  98.0 1.0 copy-done.6
  99.0 0.0 copy-start.12
  99.0 14.9 %finish.1 = bf16[3,16,32,512]{3,2,1,0:T(8,128)(2,1)S(1)} custom-call(bf16[3,16,32,512]{3,2,1,0:T(8,128)(2,1)S(1)} %copy-done, bf16[3,16,32,64]{3,2,1,0:T(8,128)(2,1)S(1)} %copy-done.3, s32[16]{0:T(128)S(1)} %copy-done.11, s32[8,1,128]{2,1,0:T(1,128)S(1)} %get-tuple-element.18.meta, f32[12,96,512]{2,1,0:T(8,128)} %get-tuple-element.19.mix_ref, ...), custom_call_target="tpu_custom_call" | custom-call | tf_op jit(solution)/shard_map/finish/pallas_call | solution.py:408
  113.9 0.0 copy-done.12
  113.9 2.0 %fusion.8 = bf16[32,3,2,8,128]{4,3,2,1,0:T(8,128)(2,1)S(1)} fusion(bf16[32,512,128]{2,1,0:T(8,128)(2,1)S(1)} %copy-done.12, bf16[3,16,32,512]{3,2,1,0:T(8,128)(2,1)S(1)} %finish.1), kind=kOutput, calls=%fused_computation.4 | convolution fusion | flops 201523200 | bytes 6160384 | tf_op jit(solution)/shard_map/srhc,hcv->srhv/dot_general | solution.py:421
  115.9 0.8 copy.41
  (5 shorter events, 0.1 us)
Async XLA Ops:
  2.2 40.1 %copy-start = (bf16[3,16,32,512]{3,2,1,0:T(8,128)(2,1)S(1)}, bf16[3,16,32,512]{3,2,1,0:T(8,128)(2,1)}, u32[]{:S(2)}) copy-start(bf16[3,16,32,512]{3,2,1,0:T(8,128)(2,1)} %query_ref.3) | copy-start | bytes 4718596
  2.2 40.1 %copy-start.3 = (bf16[3,16,32,64]{3,2,1,0:T(8,128)(2,1)S(1)}, bf16[3,16,32,64]{3,2,1,0:T(8,128)(2,1)}, u32[]{:S(2)}) copy-start(bf16[3,16,32,64]{3,2,1,0:T(8,128)(2,1)} %rotary_ref.5) | copy-start | bytes 589828
  2.2 40.1 %copy-start.8 = (bf16[3,16,128]{2,1,0:T(8,128)(2,1)S(1)}, bf16[3,16,128]{2,1,0:T(8,128)(2,1)}, u32[]{:S(2)}) copy-start(bf16[3,16,128]{2,1,0:T(8,128)(2,1)} %token_latent.1) | copy-start | bytes 36868
  2.2 40.1 %copy-start.9 = (bf16[3,16,16]{2,1,0:T(8,128)(2,1)S(1)}, bf16[3,16,16]{2,1,0:T(8,128)(2,1)}, u32[]{:S(2)}) copy-start(bf16[3,16,16]{2,1,0:T(8,128)(2,1)} %token_rotary.1) | copy-start | bytes 4612
  2.3 40.1 %copy-start.11 = (s32[16]{0:T(128)S(1)}, s32[16]{0:T(128)}, u32[]{:S(2)}) copy-start(s32[16]{0:T(128)} %lengths_ref.3) | copy-start | bytes 196
  42.4 1.4 %copy-start.2 = (bf16[12,8,64,128]{3,2,1,0:T(8,128)(2,1)S(1)}, bf16[12,8,64,128]{3,2,1,0:T(8,128)(2,1)}, u32[]{:S(2)}) copy-start(bf16[12,8,64,128]{3,2,1,0:T(8,128)(2,1)} %cache_rotary.1) | copy-start | bytes 4718596
  43.8 1.2 %copy-start.4 = (bf16[8,128,512]{2,1,0:T(8,128)(2,1)S(1)}, bf16[8,128,512]{2,1,0:T(8,128)(2,1)}, u32[]{:S(2)}) copy-start(bf16[8,128,512]{2,1,0:T(8,128)(2,1)} %get-tuple-element.15.send_latent) | copy-start | bytes 3145732
  45.0 0.9 copy-start.7
  45.9 0.7 copy-start.10
  46.6 51.4 %copy-start.1 = (bf16[32,64,128]{2,1,0:T(8,128)(2,1)S(1)}, bf16[32,64,128]{2,1,0:T(8,128)(2,1)}, u32[]{:S(2)}) copy-start(bf16[32,64,128]{2,1,0:T(8,128)(2,1)} %handed_rotary.1) | copy-start | bytes 1572868
  96.9 0.8 copy-start.5
  98.0 1.0 copy-start.6
  99.0 14.9 %copy-start.12 = (bf16[32,512,128]{2,1,0:T(8,128)(2,1)S(1)}, bf16[32,512,128]{2,1,0:T(8,128)(2,1)}, u32[]{:S(2)}) copy-start(bf16[32,512,128]{2,1,0:T(8,128)(2,1)} %param.27) | copy-start | bytes 12582916

commit v2 on v1

v2 whole, which is shorter than its diff:
```python
import functools

import jax
import jax.numpy as jnp
from jax import lax
from jax.experimental import pallas as pl
from jax.experimental.pallas import tpu as pltpu
from jax.sharding import PartitionSpec as P

GROUP = 128
FIELDS = 16
LANES = 128
MESH = pl.DeviceIdType.MESH

score_scale = 192.0 ** (-0.5)
masked_score = -1e30
VMEM_LIMIT = 48 * 1024 * 1024


def scaled(latent, rotary, exponents):
    factors = [jnp.broadcast_to(jnp.exp2(exponents[:, g:g + 1].astype(jnp.float32)).astype(jnp.bfloat16), (1, GROUP))
               for g in range(exponents.shape[1])]
    return latent * jnp.concatenate(factors[:-1], axis=1), rotary * factors[-1][:, :1]


def pack_kernel(req_dev, res_dev, request_ref, index_ref, exponent_ref, latent_ref, rotary_ref,
                send_latent, send_rotary, own_latent, own_rotary, meta, count, sems, own_sems):
    owners, rows, _ = send_latent.shape
    rot_rows = send_rotary.shape[1]
    src_blk = request_ref.shape[0]
    cap = src_blk // owners
    per_block = latent_ref.shape[1] // rows
    me, t = lax.axis_index("dp"), lax.axis_index("tp")

    @pl.loop(0, owners)
    def _(o):
        count[o] = 0
        for k in range(cap):
            for n in range(4):
                meta[o, 0, k * FIELDS + n] = 0

    @pl.loop(0, src_blk)
    def _(slot):
        request = request_ref[slot]

        @pl.when(request >= 0)
        def _():
            o = lax.div(request, req_dev)
            k = count[o]
            count[o] = k + 1
            base = k * FIELDS
            meta[o, 0, base] = 1
            meta[o, 0, base + 1] = request - o * req_dev - res_dev
            meta[o, 0, base + 2] = index_ref[slot]
            meta[o, 0, base + 3] = slot

    block = lax.div(t, per_block)
    piece = lax.rem(t, per_block)

    def send_copies(o):
        slot = meta[o, 0, block * FIELDS + 3]
        return [pltpu.make_async_copy(latent_ref.at[slot, pl.ds(pl.multiple_of(piece * rows, rows), rows)],
                                      send_latent.at[o], sems.at[o, 0]),
                pltpu.make_async_copy(
                    rotary_ref.at[slot, pl.ds(pl.multiple_of(piece * rot_rows, rot_rows), rot_rows)],
                    send_rotary.at[o], sems.at[o, 1])]

    def own_copies(k):
        slot = meta[me, 0, k * FIELDS + 3]
        return [pltpu.make_async_copy(latent_ref.at[slot], own_latent.at[k], own_sems.at[k, 0]),
                pltpu.make_async_copy(rotary_ref.at[slot], own_rotary.at[k], own_sems.at[k, 1])]

    for o in range(owners):
        for copy in send_copies(o):
            copy.start()
    for k in range(cap):
        for copy in own_copies(k):
            copy.start()
    for o in range(owners):
        for copy in send_copies(o):
            copy.wait()
        exponents = exponent_ref[pl.ds(meta[o, 0, block * FIELDS + 3], 1), :]
        send_latent[o], send_rotary[o] = scaled(send_latent[o], send_rotary[o], exponents)
    for k in range(cap):
        for copy in own_copies(k):
            copy.wait()
        exponents = exponent_ref[pl.ds(meta[me, 0, k * FIELDS + 3], 1), :]
        own_latent[k], own_rotary[k] = scaled(own_latent[k], own_rotary[k], exponents)


def attend(request, query, rotary_query, keys, rot, tokens, token_rot, length, req_dev, heads):
    nt = (((1,), (1,)), ((), ()))
    scores = lax.dot_general(query, keys, nt, preferred_element_type=jnp.float32)
    scores = (scores + jnp.dot(rotary_query, rot, preferred_element_type=jnp.float32)) * score_scale
    position = lax.broadcasted_iota(jnp.int32, (1, keys.shape[0]), 1)
    scores = jnp.where(position < length, scores, masked_score)
    fresh = (lax.dot_general(query, tokens, nt, preferred_element_type=jnp.float32)
             + lax.dot_general(rotary_query, token_rot, nt, preferred_element_type=jnp.float32)) * score_scale
    step = lax.broadcasted_iota(jnp.int32, fresh.shape, 0) // heads
    column = lax.broadcasted_iota(jnp.int32, fresh.shape, 1)
    fresh = jnp.where((lax.rem(column, req_dev) == request) & (column // req_dev <= step), fresh, masked_score)
    peak = jnp.maximum(jnp.max(scores, axis=1, keepdims=True), jnp.max(fresh, axis=1, keepdims=True))
    weights = jnp.exp(scores - peak)
    fresh = jnp.exp(fresh - peak)
    total = jnp.sum(weights, axis=1, keepdims=True) + jnp.sum(fresh, axis=1, keepdims=True)
    mix = (jnp.dot(weights.astype(jnp.bfloat16), keys, preferred_element_type=jnp.float32)
           + jnp.dot(fresh.astype(jnp.bfloat16), tokens, preferred_element_type=jnp.float32))
    return (mix / total).astype(jnp.bfloat16)


def exchange_kernel(owners, heads_groups, lengths_ref, exponent_ref, query_ref, rotary_ref,
                    cache_latent, cache_rotary, send_latent, send_rotary, send_meta, token_latent, token_rotary,
                    got_latent, got_rotary, got_meta, tokens, token_rot, mixed_ref,
                    keys, rots, queries, rot_queries, mixes, got_token, got_token_rot,
                    key_sems, mix_sems, own_sems, dp_send, dp_recv, x_send, x_recv, core_send, core_recv,
                    tok_send, tok_recv):
    me, t = lax.axis_index("dp"), lax.axis_index("tp")
    across = heads_groups // 2
    partner = t + 1 - 2 * lax.rem(t, 2)
    res_dev, blocks, block_rows, width = cache_latent.shape

    def peer(o):
        return lax.rem(me + o, owners)

    def origin(o):
        return lax.rem(me + owners - o, owners)

    def part_of(k):
        return lax.rem(t + heads_groups - 2 * k, heads_groups)

    barrier = pltpu.get_barrier_semaphore()
    for o in range(1, owners):
        pl.semaphore_signal(barrier, inc=1, device_id=(peer(o), t), device_id_type=MESH)
    for k in range(1, heads_groups):
        pl.semaphore_signal(barrier, inc=1, device_id=(me, lax.rem(t + k, heads_groups)), device_id_type=MESH)
    pl.semaphore_wait(barrier, owners - 1 + heads_groups - 1)

    def dp_copies(o):
        dst = peer(o)
        pairs = ((send_latent.at[dst], got_latent.at[me, t]), (send_rotary.at[dst], got_rotary.at[me, t]),
                 (send_meta.at[dst], got_meta.at[me]))
        return [pltpu.make_async_remote_copy(a, b, dp_send.at[o, n], dp_recv.at[o, n], device_id=(dst, t),
                                             device_id_type=MESH) for n, (a, b) in enumerate(pairs)]

    def dp_arrivals(o):
        src = origin(o)
        pairs = ((got_latent.at[src, t], 0), (got_rotary.at[src, t], 1), (got_meta.at[src], 2))
        return [pltpu.make_async_remote_copy(a, a, dp_send.at[o, n], dp_recv.at[o, n], device_id=(src, t),
                                             device_id_type=MESH) for a, n in pairs]

    def forward(o, part, to, send, recv):
        src = origin(o)
        return [pltpu.make_async_remote_copy(a.at[src, part], a.at[src, part], send.at[n], recv.at[n],
                                             device_id=(me, to), device_id_type=MESH)
                for n, a in enumerate((got_latent, got_rotary))]

    def x_copies(o, k):
        return forward(o, t, lax.rem(t + 2 * k, heads_groups), x_send.at[o, k - 1], x_recv.at[o, k - 1])

    def x_arrivals(o, k):
        return forward(o, part_of(k), part_of(k), x_send.at[o, k - 1], x_recv.at[o, k - 1])

    def core_copies(o, k):
        return forward(o, part_of(k), partner, core_send.at[o, k], core_recv.at[o, k])

    def core_arrivals(o, k):
        part = lax.rem(partner + heads_groups - 2 * k, heads_groups)
        return forward(o, part, partner, core_send.at[o, k], core_recv.at[o, k])

    def token_copies(k):
        to = lax.rem(t + k, heads_groups)
        return [pltpu.make_async_remote_copy(a, b.at[t], tok_send.at[k, n], tok_recv.at[k, n], device_id=(me, to),
                                             device_id_type=MESH)
                for n, (a, b) in enumerate(((token_latent, got_token), (token_rotary, got_token_rot)))]

    def token_arrivals(k):
        src = lax.rem(t + heads_groups - k, heads_groups)
        return [pltpu.make_async_remote_copy(b.at[src], b.at[src], tok_send.at[k, n], tok_recv.at[k, n],
                                             device_id=(me, src), device_id_type=MESH)
                for n, b in enumerate((got_token, got_token_rot))]

    def cache_copies(i, slot):
        return [pltpu.make_async_copy(cache_latent.at[i], keys.at[slot], key_sems.at[slot, 0]),
                pltpu.make_async_copy(cache_rotary.at[i], rots.at[slot], key_sems.at[slot, 1]),
                pltpu.make_async_copy(query_ref.at[:, i], queries.at[slot], key_sems.at[slot, 2]),
                pltpu.make_async_copy(rotary_ref.at[:, i], rot_queries.at[slot], key_sems.at[slot, 3])]

    def mix_copy(i, slot):
        return pltpu.make_async_copy(mixes.at[slot], mixed_ref.at[:, i], mix_sems.at[slot])

    for copy in cache_copies(0, 0):
        copy.start()
    for k in range(1, heads_groups):
        for copy in token_copies(k):
            copy.start()
    for o in range(1, owners):
        for copy in dp_copies(o):
            copy.start()
    own = [pltpu.make_async_copy(send_meta.at[me], got_meta.at[me], own_sems.at[0]),
           pltpu.make_async_copy(token_latent, got_token.at[t], own_sems.at[1]),
           pltpu.make_async_copy(token_rotary, got_token_rot.at[t], own_sems.at[2])]
    for copy in own:
        copy.start()
    for copy in own:
        copy.wait()
    for k in range(1, heads_groups):
        for copy in token_arrivals(k):
            copy.wait_recv()
    steps, req_dev = got_token.shape[1:3]
    heads = query_ref.shape[2]
    for part in range(heads_groups):
        piece, rot_piece = got_token.shape[3], got_token_rot.shape[3]
        tokens[:, part * piece:(part + 1) * piece] = got_token[part].reshape(steps * req_dev, piece)
    token_rot[...] = jnp.concatenate(
        [got_token_rot[part].reshape(steps * req_dev, got_token_rot.shape[3]) for part in range(heads_groups)], axis=1)

    def first_hop(o):
        for copy in dp_arrivals(o):
            copy.wait_recv()
        for k in range(1, across):
            for copy in x_copies(o, k):
                copy.start()
        for copy in core_copies(o, 0):
            copy.start()

    def second_hop(o):
        for k in range(1, across):
            for copy in x_arrivals(o, k):
                copy.wait_recv()
            for copy in core_copies(o, k):
                copy.start()

    first_at = {}
    second_at = {}
    for o in range(1, owners):
        first_at.setdefault(min(res_dev - 1, 2 + (o * 7) // (owners - 1)), []).append(o)
        second_at.setdefault(min(res_dev - 1, 4 + (o * 7) // (owners - 1)), []).append(o)

    @pl.loop(0, res_dev)
    def _(i):
        slot = lax.rem(i, 2)

        @pl.when(i + 1 < res_dev)
        def _():
            for copy in cache_copies(i + 1, 1 - slot):
                copy.start()

        for copy in cache_copies(i, slot):
            copy.wait()
        @pl.when(i >= 2)
        def _():
            mix_copy(i - 2, slot).wait()

        rot = []
        for j in range(blocks):
            keys[slot, j], block_rot = scaled(keys[slot, j], rots[slot, j], exponent_ref[i, pl.ds(j, 1), :])
            rot.append(block_rot)
        mixed = attend(i, queries[slot].reshape(steps * heads, width),
                       rot_queries[slot].reshape(steps * heads, rot_queries.shape[3]),
                       keys[slot].reshape(blocks * block_rows, width), jnp.concatenate(rot, axis=1),
                       tokens[...], token_rot[...], lengths_ref[i], req_dev, heads)
        mixes[slot] = mixed.reshape(steps, heads, width)
        mix_copy(i, slot).start()
        for at, hops in first_at.items():
            @pl.when(i == at)
            def _(hops=hops):
                for o in hops:
                    first_hop(o)
        for at, hops in second_at.items():
            @pl.when(i == at)
            def _(hops=hops):
                for o in hops:
                    second_hop(o)

    for i in range(max(res_dev - 2, 0), res_dev):
        mix_copy(i, i % 2).wait()
    for k in range(1, heads_groups):
        for copy in token_copies(k):
            copy.wait_send()
    for o in range(1, owners):
        for copy in dp_copies(o):
            copy.wait_send()
        for k in range(1, across):
            for copy in x_copies(o, k):
                copy.wait_send()
        for k in range(across):
            for copy in core_copies(o, k):
                copy.wait_send()
            for copy in core_arrivals(o, k):
                copy.wait_recv()


def finish_kernel(lengths_ref, meta, tokens, token_rot, query_ref, rotary_ref, own_latent, own_rotary,
                  got_latent, got_rotary, partly_mixed, mixed_ref, keys, rots, queries, rot_queries, mixes, sems, query_sems,
                  mix_sems):
    me = lax.axis_index("dp")
    hand, blocks, block_rows, width = keys.shape
    owners, groups, rows, _ = got_latent.shape
    rot_rows = got_rotary.shape[2]
    per_block = block_rows // rows
    cap = groups // per_block
    steps, req_dev, heads, _ = query_ref.shape
    res_dev = req_dev - hand

    def query_copies(i):
        return [pltpu.make_async_copy(query_ref.at[:, res_dev + i], queries.at[i], query_sems.at[i, 0]),
                pltpu.make_async_copy(rotary_ref.at[:, res_dev + i], rot_queries.at[i], query_sems.at[i, 1])]

    for i in range(hand):
        for copy in query_copies(i):
            copy.start()
    keys[...] = jnp.zeros_like(keys)
    rots[...] = jnp.zeros_like(rots)

    def each_copy(act):
        @pl.loop(0, owners)
        def _(d):
            for k in range(cap):
                base = k * FIELDS

                @pl.when(meta[d, 0, base] == 1)
                def _(k=k, base=base):
                    i, b = meta[d, 0, base + 1], meta[d, 0, base + 2]
                    for p in range(per_block):
                        part = k * per_block + p
                        to_keys = keys.at[i, b, pl.ds(p * rows, rows)]
                        to_rots = rots.at[i, b, pl.ds(p * rot_rows, rot_rows)]

                        @pl.when(d == me)
                        def _():
                            act(pltpu.make_async_copy(own_latent.at[k, pl.ds(p * rows, rows)], to_keys,
                                                      sems.at[d, part, 0]))
                            act(pltpu.make_async_copy(own_rotary.at[k, pl.ds(p * rot_rows, rot_rows)], to_rots,
                                                      sems.at[d, part, 1]))

                        @pl.when(d != me)
                        def _():
                            act(pltpu.make_async_copy(got_latent.at[d, part], to_keys, sems.at[d, part, 0]))
                            act(pltpu.make_async_copy(got_rotary.at[d, part], to_rots, sems.at[d, part, 1]))

    each_copy(lambda copy: copy.start())
    for i in range(hand):
        for copy in query_copies(i):
            copy.wait()
    each_copy(lambda copy: copy.wait())

    def mix_copy(i):
        return pltpu.make_async_copy(mixes.at[i], mixed_ref.at[:, res_dev + i], mix_sems.at[i])

    @pl.loop(0, hand)
    def _(i):
        mixed = attend(res_dev + i, queries[i].reshape(steps * heads, width),
                       rot_queries[i].reshape(steps * heads, rot_queries.shape[3]),
                       keys[i].reshape(blocks * block_rows, width),
                       jnp.concatenate([rots[i, j] for j in range(blocks)], axis=1),
                       tokens[...], token_rot[...], lengths_ref[res_dev + i], req_dev, heads)
        mixes[i] = mixed.reshape(steps, heads, width)
        mix_copy(i).start()

    for i in range(hand):
        mix_copy(i).wait()


def local(
    query_latent,
    query_rotary,
    token_latent,
    token_rotary,
    cache_latent,
    cache_rotary,
    cache_exponent,
    handed_latent,
    handed_rotary,
    handed_exponent,
    block_request,
    block_index,
    lengths,
    value_up,
):
    owners, groups = lax.axis_size("dp"), lax.axis_size("tp")
    req_dev = lengths.shape[0]
    res_dev, blocks, block_rows, width = cache_latent.shape
    rot_width = cache_rotary.shape[2]
    hand = req_dev - res_dev
    src_blk = block_request.shape[0]
    cap = src_blk // owners
    steps, _, heads, _ = query_latent.shape
    rows, rot_rows = cap * block_rows // groups, cap * rot_width // groups
    across = groups // 2
    bf16, f32 = jnp.bfloat16, jnp.float32
    shape = jax.ShapeDtypeStruct
    hbm, vmem, smem = (pl.BlockSpec(memory_space=m) for m in (pl.ANY, pltpu.VMEM, pltpu.SMEM))
    dma = pltpu.SemaphoreType.DMA

    send_latent, send_rotary, own_latent, own_rotary, send_meta = pl.pallas_call(
        functools.partial(pack_kernel, req_dev, res_dev),
        out_shape=[shape((owners, rows, width), bf16), shape((owners, rot_rows, block_rows), bf16),
                   shape((cap, block_rows, width), bf16), shape((cap, rot_width, block_rows), bf16),
                   shape((owners, 1, LANES), jnp.int32)],
        in_specs=[smem, smem, vmem, hbm, hbm],
        out_specs=[vmem, vmem, vmem, vmem, smem],
        scratch_shapes=[pltpu.SMEM((owners,), jnp.int32), dma((owners, 2)), dma((cap, 2))],
        compiler_params=pltpu.CompilerParams(vmem_limit_bytes=VMEM_LIMIT),
        name="pack",
    )(block_request, block_index, handed_exponent, handed_latent, handed_rotary)

    got_latent, got_rotary, got_meta, tokens, token_rot, mixed = pl.pallas_call(
        functools.partial(exchange_kernel, owners, groups),
        out_shape=[shape((owners, groups, rows, width), bf16), shape((owners, groups, rot_rows, block_rows), bf16),
                   shape((owners, 1, LANES), jnp.int32), shape((steps * req_dev, width), bf16),
                   shape((steps * req_dev, query_rotary.shape[3]), bf16), shape((steps, req_dev, heads, width), bf16)],
        in_specs=[smem, vmem] + [hbm] * 9,
        out_specs=[vmem, vmem, vmem, vmem, vmem, hbm],
        scratch_shapes=[pltpu.VMEM((2, blocks, block_rows, width), bf16),
                        pltpu.VMEM((2, blocks, rot_width, block_rows), bf16),
                        pltpu.VMEM((2, steps, heads, width), bf16),
                        pltpu.VMEM((2, steps, heads, query_rotary.shape[3]), bf16),
                        pltpu.VMEM((2, steps, heads, width), bf16),
                        pltpu.VMEM((groups,) + token_latent.shape, bf16),
                        pltpu.VMEM((groups,) + token_rotary.shape, bf16),
                        dma((2, 4)), dma((2,)), dma((3,)), dma((owners, 3)), dma((owners, 3)),
                        dma((owners, across - 1, 2)), dma((owners, across - 1, 2)),
                        dma((owners, across, 2)), dma((owners, across, 2)),
                        dma((groups, 2)), dma((groups, 2))],
        compiler_params=pltpu.CompilerParams(collective_id=0, has_side_effects=True, vmem_limit_bytes=VMEM_LIMIT),
        name="exchange",
    )(lengths, cache_exponent, query_latent, query_rotary, cache_latent, cache_rotary, send_latent, send_rotary,
      send_meta, token_latent, token_rotary)

    mixed = pl.pallas_call(
        finish_kernel,
        out_shape=shape((steps, req_dev, heads, width), bf16),
        in_specs=[smem, smem, vmem, vmem] + [hbm] * 7,
        out_specs=hbm,
        input_output_aliases={10: 0},
        scratch_shapes=[pltpu.VMEM((hand, blocks, block_rows, width), bf16),
                        pltpu.VMEM((hand, blocks, rot_width, block_rows), bf16),
                        pltpu.VMEM((hand, steps, heads, width), bf16),
                        pltpu.VMEM((hand, steps, heads, query_rotary.shape[3]), bf16),
                        pltpu.VMEM((hand, steps, heads, width), bf16),
                        dma((owners, groups, 2)), dma((hand, 2)), dma((hand,))],
        compiler_params=pltpu.CompilerParams(vmem_limit_bytes=VMEM_LIMIT),
        name="finish",
    )(lengths, got_meta, tokens, token_rot, query_latent, query_rotary, own_latent, own_rotary, got_latent, got_rotary,
      mixed)

    output = jnp.einsum("srhc,hcv->srhv", mixed, value_up, preferred_element_type=f32).astype(bf16)
    return output.reshape(steps, req_dev, -1)


def solution(mesh):
    placed = (
        P(None, "dp", "tp", None),
        P(None, "dp", "tp", None),
        P(None, "dp", "tp"),
        P(None, "dp", "tp"),
        P("dp", None, None, None),
        P("dp", None, None, None),
        P("dp", None, None),
        P("dp", None, None),
        P("dp", None, None),
        P("dp", None),
        P("dp"),
        P("dp"),
        P("dp"),
        P("tp", None, None),
    )
    return jax.shard_map(
        local, mesh=mesh, in_specs=placed, out_specs=P(None, "dp", "tp"), check_vma=False
    )
```

time: 118 us -> 69 us (0.58)
  Pallas kernels: 105 us -> 61.8 us
  local copies, waits for them, and re-layouts: 9.34 us -> 4.82 us
    pallas_call x1, Pallas kernels: 40 us -> 4.6 us  [local(): pl.pallas_call(functools.partial(pack_kernel, req_dev, res_dev), out_shap...]
    pallas_call x1, Pallas kernels: 14.9 us -> 7.83 us  [local(): pl.pallas_call(finish_kernel, out_shape=shape((steps, req_dev, heads, wid...]
    unnamed x28 -> x20, local copies, waits for them, and re-layouts: 8.31 us -> 4 us
where the time goes in v2:
time: 69 us; the launch traced here: 68.7 us
  Pallas kernels  61.8 us (90%)
  local copies, waits for them, and re-layouts  4.82 us (7%)
  matrix products  1.96 us (3%)
    pallas_call x1, Pallas kernels, local(): pl.pallas_call(functools.partial(exchange_kernel, owners, groups), out_sh...  49.4 us
    pallas_call x1, Pallas kernels, local(): pl.pallas_call(finish_kernel, out_shape=shape((steps, req_dev, heads, wid...  7.83 us
    pallas_call x1, Pallas kernels, local(): pl.pallas_call(functools.partial(pack_kernel, req_dev, res_dev), out_shap...  4.6 us
    unnamed x20, local copies, waits for them, and re-layouts  4 us
    dot_general x1, matrix products, local(): jnp.einsum('srhc,hcv->srhv', mixed, value_up, preferred_element_type=f32)  1.96 us

profile of v2, /device:TPU:25, one launch (start us, length us, event | category | flops | bytes accessed | tf_op | source)
XLA Modules:
  0.0 68.7 jit_solution(10670266717351802684)
XLA Ops:
  0.0 0.8 %copy.19.exponent_ref = s32[32,5]{1,0:T(8,128)S(1)} copy(s32[32,5]{0,1:T(8,128)} %param.23) | data formatting | bytes 1280 | tf_op args[9]
  0.8 0.9 %copy.20.exponent_ref = s32[12,8,5]{2,1,0:T(8,128)S(1)} copy(s32[12,8,5]{0,1,2:T(8,128)} %param.20) | data formatting | bytes 3840 | tf_op args[6]
  1.6 0.0 copy-start.2
  1.6 1.0 %copy-done.2 = bf16[32,64,128]{2,1,0:T(8,128)(2,1)S(1)} copy-done((bf16[32,64,128]{2,1,0:T(8,128)(2,1)S(1)}, bf16[32,64,128]{2,1,0:T(8,128)(2,1)}, u32[]{:S(2)}) %copy-start.2) | copy-done | bytes 524312
  2.7 0.0 copy-start.6
  2.7 0.7 copy-done.6
  3.3 0.0 copy-start.7
  3.3 0.7 copy-done.7
  4.0 0.0 copy-start
  4.0 0.0 copy-start.1
  4.0 0.0 copy-start.3
  4.0 0.0 copy-start.4
  4.0 0.0 copy-start.5
  4.0 4.6 %pack.1 = (bf16[8,128,512]{2,1,0:T(8,128)(2,1)S(1)}, bf16[8,64,128]{2,1,0:T(8,128)(2,1)S(1)}, bf16[4,128,512]{2,1,0:T(8,128)(2,1)S(1)}, bf16[4,64,128]{2,1,0:T(8,128)(2,1)S(1)}, s32[8,1,128]{2,1,0:T(1,128)S(1)}) custom-call(s32[32]{0:T(128)S(1)} %copy-done.6, s32[32]{0:T(128)S(1)} %copy-done.7, s32[32,5]{1,0:T(8,128)S(1)} %copy.19.exponent_ref, ...), custom_call_target="tpu_custom_call" | custom-call | tf_op jit(solution)/shard_map/pack/pallas_call | solution.py:395
  8.6 0.0 copy-done
  8.6 0.0 copy-done.1
  8.6 0.0 copy-done.3
  8.6 0.0 copy-done.4
  8.7 0.0 copy-done.5
  8.7 49.4 %exchange.1 = (bf16[8,4,128,512]{3,2,1,0:T(8,128)(2,1)}, bf16[8,4,64,128]{3,2,1,0:T(8,128)(2,1)S(1)}, s32[8,1,128]{2,1,0:T(1,128)S(1)}, bf16[48,512]{1,0:T(8,128...) custom-call(s32[16]{0:T(128)S(1)} %copy-done.5, s32[12,8,5]{2,1,0:T(8,128)S(1)} %copy.20.exponent_ref, ...), custom_call_target="tpu_custom_call" | custom-call | tf_op jit(solution)/shard_map/exchange/pallas_call | solution.py:407
  58.1 0.0 copy-start.8
  58.1 7.8 %finish.1 = bf16[3,16,32,512]{3,2,1,0:T(8,128)(2,1)S(1)} custom-call(s32[16]{0:T(128)S(1)} %copy-done.5, s32[8,1,128]{2,1,0:T(1,128)S(1)} %get-tuple-element.19.meta, bf16[48,512]{1,0:T(8,128)(2,1)S(1)} %get-tuple-element.20.tokens, bf16[48,64]{1,0:T(8,128)(2,1)S(1)} %get-tuple-element.21.token_rot, ...), custom_call_target="tpu_custom_call", output_to_operand_aliasing={{}: (10, {})} | custom-call | tf_op jit(solution)/shard_map/finish/pallas_call | solution.py:430
  65.9 0.0 copy-done.8
  65.9 2.0 %fusion.8 = bf16[32,3,2,8,128]{4,3,2,1,0:T(8,128)(2,1)S(1)} fusion(bf16[32,512,128]{2,1,0:T(8,128)(2,1)S(1)} %copy-done.8, bf16[3,16,32,512]{3,2,1,0:T(8,128)(2,1)S(1)} %finish.1), kind=kOutput, calls=%fused_computation.4 | convolution fusion | flops 201523200 | bytes 6160384 | tf_op jit(solution)/shard_map/srhc,hcv->srhv/dot_general | solution.py:447
  67.9 0.8 %copy.32 = bf16[32,3,2,8,128]{4,3,0,2,1:T(8,128)(2,1)} copy(bf16[32,3,2,8,128]{4,3,2,1,0:T(8,128)(2,1)S(1)} %fusion.8) | data formatting | bytes 786432 | tf_op jit(solution)/shard_map/reshape | solution.py:448
Async XLA Ops:
  1.6 1.0 %copy-start.2 = (bf16[32,64,128]{2,1,0:T(8,128)(2,1)S(1)}, bf16[32,64,128]{2,1,0:T(8,128)(2,1)}, u32[]{:S(2)}) copy-start(bf16[32,64,128]{2,1,0:T(8,128)(2,1)} %rotary_ref.3) | copy-start | bytes 1572868
  2.7 0.7 copy-start.6
  3.3 0.7 copy-start.7
  4.0 4.6 %copy-start = (bf16[3,16,32,512]{3,2,1,0:T(8,128)(2,1)S(1)}, bf16[3,16,32,512]{3,2,1,0:T(8,128)(2,1)}, u32[]{:S(2)}) copy-start(bf16[3,16,32,512]{3,2,1,0:T(8,128)(2,1)} %query_ref.3) | copy-start | bytes 4718596
  4.0 4.6 %copy-start.1 = (bf16[3,16,32,64]{3,2,1,0:T(8,128)(2,1)S(1)}, bf16[3,16,32,64]{3,2,1,0:T(8,128)(2,1)}, u32[]{:S(2)}) copy-start(bf16[3,16,32,64]{3,2,1,0:T(8,128)(2,1)} %rotary_ref.5) | copy-start | bytes 589828
  4.0 4.7 %copy-start.3 = (bf16[3,16,128]{2,1,0:T(8,128)(2,1)S(1)}, bf16[3,16,128]{2,1,0:T(8,128)(2,1)}, u32[]{:S(2)}) copy-start(bf16[3,16,128]{2,1,0:T(8,128)(2,1)} %token_latent.1) | copy-start | bytes 36868
  4.0 4.7 %copy-start.4 = (bf16[3,16,16]{2,1,0:T(8,128)(2,1)S(1)}, bf16[3,16,16]{2,1,0:T(8,128)(2,1)}, u32[]{:S(2)}) copy-start(bf16[3,16,16]{2,1,0:T(8,128)(2,1)} %token_rotary.1) | copy-start | bytes 4612
  4.0 4.7 %copy-start.5 = (s32[16]{0:T(128)S(1)}, s32[16]{0:T(128)}, u32[]{:S(2)}) copy-start(s32[16]{0:T(128)} %lengths_ref.3) | copy-start | bytes 196
  58.1 7.9 %copy-start.8 = (bf16[32,512,128]{2,1,0:T(8,128)(2,1)S(1)}, bf16[32,512,128]{2,1,0:T(8,128)(2,1)}, u32[]{:S(2)}) copy-start(bf16[32,512,128]{2,1,0:T(8,128)(2,1)} %param.27) | copy-start | bytes 12582916

commit v3 on v2

--- a/solution.py
+++ b/solution.py
@@ -11,6 +11,22 @@
 FIELDS = 16
 LANES = 128
 MESH = pl.DeviceIdType.MESH
+
+PIECES = 4
+ROUNDS_AHEAD = 2
+FIRST_EVENT = 3
+EVENT_STEP = 3
+RING = 4
+
+
+def FLOW_ORDER(owners):
+    low = owners // RING
+    order = []
+    for side in range(low):
+        for turn, ring in enumerate((2, 1, 3, 0)):
+            order.append(ring * low + (side + turn) % low)
+    return [o for o in order if o > 0]
+
 
 score_scale = 192.0 ** (-0.5)
 masked_score = -1e30
@@ -119,11 +135,17 @@
     partner = t + 1 - 2 * lax.rem(t, 2)
     res_dev, blocks, block_rows, width = cache_latent.shape
 
+    low = owners // RING
+
+    def shifted(o, sign):
+        ring, side = o // low, o % low
+        return lax.rem(lax.div(me, low) + RING + sign * ring, RING) * low + lax.rem(me + low + sign * side, low)
+
     def peer(o):
-        return lax.rem(me + o, owners)
+        return shifted(o, 1)
 
     def origin(o):
-        return lax.rem(me + owners - o, owners)
+        return shifted(o, -1)
 
     def part_of(k):
         return lax.rem(t + heads_groups - 2 * k, heads_groups)
@@ -135,18 +157,26 @@
         pl.semaphore_signal(barrier, inc=1, device_id=(me, lax.rem(t + k, heads_groups)), device_id_type=MESH)
     pl.semaphore_wait(barrier, owners - 1 + heads_groups - 1)
 
-    def dp_copies(o):
+    rows = send_latent.shape[1]
+    pieces = min(PIECES, rows // 16)
+    step_rows = rows // pieces
+
+    def dp_copies(o, p):
         dst = peer(o)
-        pairs = ((send_latent.at[dst], got_latent.at[me, t]), (send_rotary.at[dst], got_rotary.at[me, t]),
-                 (send_meta.at[dst], got_meta.at[me]))
+        cut = pl.ds(p * step_rows, step_rows)
+        pairs = [(send_latent.at[dst, cut], got_latent.at[me, t, cut], p)]
+        if p == 0:
+            pairs += [(send_rotary.at[dst], got_rotary.at[me, t], pieces), (send_meta.at[dst], got_meta.at[me], pieces + 1)]
         return [pltpu.make_async_remote_copy(a, b, dp_send.at[o, n], dp_recv.at[o, n], device_id=(dst, t),
-                                             device_id_type=MESH) for n, (a, b) in enumerate(pairs)]
-
-    def dp_arrivals(o):
+                                             device_id_type=MESH) for a, b, n in pairs]
+
+    def dp_arrivals(o, p):
         src = origin(o)
-        pairs = ((got_latent.at[src, t], 0), (got_rotary.at[src, t], 1), (got_meta.at[src], 2))
+        landed = [(got_latent.at[src, t, pl.ds(p * step_rows, step_rows)], p)]
+        if p == 0:
+            landed += [(got_rotary.at[src, t], pieces), (got_meta.at[src], pieces + 1)]
         return [pltpu.make_async_remote_copy(a, a, dp_send.at[o, n], dp_recv.at[o, n], device_id=(src, t),
-                                             device_id_type=MESH) for a, n in pairs]
+                                             device_id_type=MESH) for a, n in landed]
 
     def forward(o, part, to, send, recv):
         src = origin(o)
@@ -154,11 +184,19 @@
                                              device_id=(me, to), device_id_type=MESH)
                 for n, a in enumerate((got_latent, got_rotary))]
 
-    def x_copies(o, k):
-        return forward(o, t, lax.rem(t + 2 * k, heads_groups), x_send.at[o, k - 1], x_recv.at[o, k - 1])
-
-    def x_arrivals(o, k):
-        return forward(o, part_of(k), part_of(k), x_send.at[o, k - 1], x_recv.at[o, k - 1])
+    def x_forward(o, k, p, part, to):
+        src = origin(o)
+        moved = [(got_latent.at[src, part, pl.ds(p * step_rows, step_rows)], p)]
+        if p == 0:
+            moved.append((got_rotary.at[src, part], pieces))
+        return [pltpu.make_async_remote_copy(a, a, x_send.at[o, k - 1, n], x_recv.at[o, k - 1, n], device_id=(me, to),
+                                             device_id_type=MESH) for a, n in moved]
+
+    def x_copies(o, k, p):
+        return x_forward(o, k, p, t, lax.rem(t + 2 * k, heads_groups))
+
+    def x_arrivals(o, k, p):
+        return x_forward(o, k, p, part_of(k), part_of(k))
 
     def core_copies(o, k):
         return forward(o, part_of(k), partner, core_send.at[o, k], core_recv.at[o, k])
@@ -193,9 +231,11 @@
     for k in range(1, heads_groups):
         for copy in token_copies(k):
             copy.start()
-    for o in range(1, owners):
-        for copy in dp_copies(o):
-            copy.start()
+    order = FLOW_ORDER(owners)
+    for p in range(min(ROUNDS_AHEAD, pieces)):
+        for o in order:
+            for copy in dp_copies(o, p):
+                copy.start()
     own = [pltpu.make_async_copy(send_meta.at[me], got_meta.at[me], own_sems.at[0]),
            pltpu.make_async_copy(token_latent, got_token.at[t], own_sems.at[1]),
            pltpu.make_async_copy(token_rotary, got_token_rot.at[t], own_sems.at[2])]
@@ -214,27 +254,25 @@
     token_rot[...] = jnp.concatenate(
         [got_token_rot[part].reshape(steps * req_dev, got_token_rot.shape[3]) for part in range(heads_groups)], axis=1)
 
-    def first_hop(o):
-        for copy in dp_arrivals(o):
-            copy.wait_recv()
-        for k in range(1, across):
-            for copy in x_copies(o, k):
-                copy.start()
-        for copy in core_copies(o, 0):
-            copy.start()
-
-    def second_hop(o):
-        for k in range(1, across):
-            for copy in x_arrivals(o, k):
+    def arrive(p):
+        for o in order:
+            for copy in dp_arrivals(o, p):
                 copy.wait_recv()
-            for copy in core_copies(o, k):
-                copy.start()
-
-    first_at = {}
-    second_at = {}
-    for o in range(1, owners):
-        first_at.setdefault(min(res_dev - 1, 2 + (o * 7) // (owners - 1)), []).append(o)
-        second_at.setdefault(min(res_dev - 1, 4 + (o * 7) // (owners - 1)), []).append(o)
+            for k in range(1, across):
+                for copy in x_copies(o, k, p):
+                    copy.start()
+            for copy in dp_copies(o, p):
+                copy.wait_send()
+            if p + ROUNDS_AHEAD < pieces:
+                for copy in dp_copies(o, p + ROUNDS_AHEAD):
+                    copy.start()
+            if p == pieces - 1:
+                for copy in core_copies(o, 0):
+                    copy.start()
+
+    events = {}
+    for p in range(pieces):
+        events.setdefault(min(FIRST_EVENT + p * EVENT_STEP, res_dev), []).append(p)
 
     @pl.loop(0, res_dev)
     def _(i):
@@ -261,28 +299,32 @@
                        tokens[...], token_rot[...], lengths_ref[i], req_dev, heads)
         mixes[slot] = mixed.reshape(steps, heads, width)
         mix_copy(i, slot).start()
-        for at, hops in first_at.items():
-            @pl.when(i == at)
-            def _(hops=hops):
-                for o in hops:
-                    first_hop(o)
-        for at, hops in second_at.items():
-            @pl.when(i == at)
-            def _(hops=hops):
-                for o in hops:
-                    second_hop(o)
-
+        for at, due in events.items():
+            if at < res_dev:
+                @pl.when(i == at)
+                def _(due=due):
+                    for p in due:
+                        arrive(p)
+
+    for p in events.get(res_dev, []):
+        arrive(p)
+    for o in order:
+        for k in range(1, across):
+            for p in range(pieces):
+                for copy in x_arrivals(o, k, p):
+                    copy.wait_recv()
+            for copy in core_copies(o, k):
+                copy.start()
     for i in range(max(res_dev - 2, 0), res_dev):
         mix_copy(i, i % 2).wait()
     for k in range(1, heads_groups):
         for copy in token_copies(k):
             copy.wait_send()
     for o in range(1, owners):
-        for copy in dp_copies(o):
-            copy.wait_send()
         for k in range(1, across):
-            for copy in x_copies(o, k):
-                copy.wait_send()
+            for p in range(pieces):
+                for copy in x_copies(o, k, p):
+                    copy.wait_send()
         for k in range(across):
             for copy in core_copies(o, k):
                 copy.wait_send()
@@ -418,8 +460,8 @@
                         pltpu.VMEM((2, steps, heads, width), bf16),
                         pltpu.VMEM((groups,) + token_latent.shape, bf16),
                         pltpu.VMEM((groups,) + token_rotary.shape, bf16),
-                        dma((2, 4)), dma((2,)), dma((3,)), dma((owners, 3)), dma((owners, 3)),
-                        dma((owners, across - 1, 2)), dma((owners, across - 1, 2)),
+                        dma((2, 4)), dma((2,)), dma((3,)), dma((owners, PIECES + 2)), dma((owners, PIECES + 2)),
+                        dma((owners, across - 1, min(PIECES, rows // 16) + 1)), dma((owners, across - 1, min(PIECES, rows // 16) + 1)),
                         dma((owners, across, 2)), dma((owners, across, 2)),
                         dma((groups, 2)), dma((groups, 2))],
         compiler_params=pltpu.CompilerParams(collective_id=0, has_side_effects=True, vmem_limit_bytes=VMEM_LIMIT),

time: 69 us -> 64.9 us (0.941)
  the two profiles are of different devices: /device:TPU:25 before, /device:TPU:13 now
where the time goes in v3:
time: 64.9 us; the launch traced here: 64.8 us
  Pallas kernels  57.9 us (89%)
  local copies, waits for them, and re-layouts  4.82 us (7%)
  matrix products  1.96 us (3%)
    pallas_call x1, Pallas kernels, local(): pl.pallas_call(functools.partial(exchange_kernel, owners, groups), out_sh...  45.3 us
    pallas_call x1, Pallas kernels, local(): pl.pallas_call(finish_kernel, out_shape=shape((steps, req_dev, heads, wid...  8.03 us
    pallas_call x1, Pallas kernels, local(): pl.pallas_call(functools.partial(pack_kernel, req_dev, res_dev), out_shap...  4.6 us
    unnamed x20, local copies, waits for them, and re-layouts  4 us
    dot_general x1, matrix products, local(): jnp.einsum('srhc,hcv->srhv', mixed, value_up, preferred_element_type=f32)  1.96 us

profile of v3, /device:TPU:13, one launch (start us, length us, event | category | flops | bytes accessed | tf_op | source)
XLA Modules:
  0.0 64.8 jit_solution(11999428753465629028)
XLA Ops:
  0.0 0.8 %copy.19.exponent_ref = s32[32,5]{1,0:T(8,128)S(1)} copy(s32[32,5]{0,1:T(8,128)} %param.23) | data formatting | bytes 1280 | tf_op args[9]
  0.8 0.9 %copy.20.exponent_ref = s32[12,8,5]{2,1,0:T(8,128)S(1)} copy(s32[12,8,5]{0,1,2:T(8,128)} %param.20) | data formatting | bytes 3840 | tf_op args[6]
  1.6 0.0 copy-start.2
  1.6 1.0 %copy-done.2 = bf16[32,64,128]{2,1,0:T(8,128)(2,1)S(1)} copy-done((bf16[32,64,128]{2,1,0:T(8,128)(2,1)S(1)}, bf16[32,64,128]{2,1,0:T(8,128)(2,1)}, u32[]{:S(2)}) %copy-start.2) | copy-done | bytes 524312
  2.7 0.0 copy-start.6
  2.7 0.7 %copy-done.6 = s32[32]{0:T(128)S(1)} copy-done((s32[32]{0:T(128)S(1)}, s32[32]{0:T(128)}, u32[]{:S(2)}) %copy-start.6) | copy-done | bytes 152
  3.3 0.0 copy-start.7
  3.3 0.7 %copy-done.7 = s32[32]{0:T(128)S(1)} copy-done((s32[32]{0:T(128)S(1)}, s32[32]{0:T(128)}, u32[]{:S(2)}) %copy-start.7) | copy-done | bytes 152
  4.0 0.0 copy-start
  4.0 0.0 copy-start.1
  4.0 0.0 copy-start.3
  4.0 0.0 copy-start.4
  4.0 0.0 copy-start.5
  4.0 4.6 %pack.1 = (bf16[8,128,512]{2,1,0:T(8,128)(2,1)S(1)}, bf16[8,64,128]{2,1,0:T(8,128)(2,1)S(1)}, bf16[4,128,512]{2,1,0:T(8,128)(2,1)S(1)}, bf16[4,64,128]{2,1,0:T(8,128)(2,1)S(1)}, s32[8,1,128]{2,1,0:T(1,128)S(1)}) custom-call(s32[32]{0:T(128)S(1)} %copy-done.6, s32[32]{0:T(128)S(1)} %copy-done.7, s32[32,5]{1,0:T(8,128)S(1)} %copy.19.exponent_ref, ...), custom_call_target="tpu_custom_call" | custom-call | tf_op jit(solution)/shard_map/pack/pallas_call | solution.py:437
  8.6 0.0 copy-done
  8.6 0.0 copy-done.1
  8.6 0.0 copy-done.3
  8.6 0.0 copy-done.4
  8.7 0.0 copy-done.5
  8.7 45.3 %exchange.1 = (bf16[8,4,128,512]{3,2,1,0:T(8,128)(2,1)}, bf16[8,4,64,128]{3,2,1,0:T(8,128)(2,1)S(1)}, s32[8,1,128]{2,1,0:T(1,128)S(1)}, bf16[48,512]{1,0:T(8,128...) custom-call(s32[16]{0:T(128)S(1)} %copy-done.5, s32[12,8,5]{2,1,0:T(8,128)S(1)} %copy.20.exponent_ref, ...), custom_call_target="tpu_custom_call" | custom-call | tf_op jit(solution)/shard_map/exchange/pallas_call | solution.py:449
  53.9 0.0 copy-start.8
  54.0 8.0 %finish.1 = bf16[3,16,32,512]{3,2,1,0:T(8,128)(2,1)S(1)} custom-call(s32[16]{0:T(128)S(1)} %copy-done.5, s32[8,1,128]{2,1,0:T(1,128)S(1)} %get-tuple-element.19.meta, bf16[48,512]{1,0:T(8,128)(2,1)S(1)} %get-tuple-element.20.tokens, bf16[48,64]{1,0:T(8,128)(2,1)S(1)} %get-tuple-element.21.token_rot, ...), custom_call_target="tpu_custom_call", output_to_operand_aliasing={{}: (10, {})} | custom-call | tf_op jit(solution)/shard_map/finish/pallas_call | solution.py:472
  62.0 0.0 copy-done.8
  62.0 2.0 %fusion.8 = bf16[32,3,2,8,128]{4,3,2,1,0:T(8,128)(2,1)S(1)} fusion(bf16[32,512,128]{2,1,0:T(8,128)(2,1)S(1)} %copy-done.8, bf16[3,16,32,512]{3,2,1,0:T(8,128)(2,1)S(1)} %finish.1), kind=kOutput, calls=%fused_computation.4 | convolution fusion | flops 201523200 | bytes 6160384 | tf_op jit(solution)/shard_map/srhc,hcv->srhv/dot_general | solution.py:489
  64.0 0.8 %copy.32 = bf16[32,3,2,8,128]{4,3,0,2,1:T(8,128)(2,1)} copy(bf16[32,3,2,8,128]{4,3,2,1,0:T(8,128)(2,1)S(1)} %fusion.8) | data formatting | bytes 786432 | tf_op jit(solution)/shard_map/reshape | solution.py:490
Async XLA Ops:
  1.6 1.0 %copy-start.2 = (bf16[32,64,128]{2,1,0:T(8,128)(2,1)S(1)}, bf16[32,64,128]{2,1,0:T(8,128)(2,1)}, u32[]{:S(2)}) copy-start(bf16[32,64,128]{2,1,0:T(8,128)(2,1)} %rotary_ref.3) | copy-start | bytes 1572868
  2.7 0.7 %copy-start.6 = (s32[32]{0:T(128)S(1)}, s32[32]{0:T(128)}, u32[]{:S(2)}) copy-start(s32[32]{0:T(128)} %request_ref.1) | copy-start | bytes 388
  3.3 0.7 %copy-start.7 = (s32[32]{0:T(128)S(1)}, s32[32]{0:T(128)}, u32[]{:S(2)}) copy-start(s32[32]{0:T(128)} %index_ref.1) | copy-start | bytes 388
  4.0 4.6 %copy-start = (bf16[3,16,32,512]{3,2,1,0:T(8,128)(2,1)S(1)}, bf16[3,16,32,512]{3,2,1,0:T(8,128)(2,1)}, u32[]{:S(2)}) copy-start(bf16[3,16,32,512]{3,2,1,0:T(8,128)(2,1)} %query_ref.3) | copy-start | bytes 4718596
  4.0 4.6 %copy-start.1 = (bf16[3,16,32,64]{3,2,1,0:T(8,128)(2,1)S(1)}, bf16[3,16,32,64]{3,2,1,0:T(8,128)(2,1)}, u32[]{:S(2)}) copy-start(bf16[3,16,32,64]{3,2,1,0:T(8,128)(2,1)} %rotary_ref.5) | copy-start | bytes 589828
  4.0 4.7 %copy-start.3 = (bf16[3,16,128]{2,1,0:T(8,128)(2,1)S(1)}, bf16[3,16,128]{2,1,0:T(8,128)(2,1)}, u32[]{:S(2)}) copy-start(bf16[3,16,128]{2,1,0:T(8,128)(2,1)} %token_latent.1) | copy-start | bytes 36868
  4.0 4.7 %copy-start.4 = (bf16[3,16,16]{2,1,0:T(8,128)(2,1)S(1)}, bf16[3,16,16]{2,1,0:T(8,128)(2,1)}, u32[]{:S(2)}) copy-start(bf16[3,16,16]{2,1,0:T(8,128)(2,1)} %token_rotary.1) | copy-start | bytes 4612
  4.0 4.7 %copy-start.5 = (s32[16]{0:T(128)S(1)}, s32[16]{0:T(128)}, u32[]{:S(2)}) copy-start(s32[16]{0:T(128)} %lengths_ref.3) | copy-start | bytes 196
  53.9 8.0 %copy-start.8 = (bf16[32,512,128]{2,1,0:T(8,128)(2,1)S(1)}, bf16[32,512,128]{2,1,0:T(8,128)(2,1)}, u32[]{:S(2)}) copy-start(bf16[32,512,128]{2,1,0:T(8,128)(2,1)} %param.27) | copy-start | bytes 12582916
